TPU v7x, 512 devices: a whole 4x8x8 slice. The times are simulated.
512 devices in a mesh: term: 8 (over y), sector: 64 (over x, z, core).
Axes of the slice: x: 4, y: 8, z: 8, core: 2. Of those that a mesh axis runs over, the one named last changes fastest.
Arguments:
- psi: float32 [4096, 32, 128], P('sector'), may hold values from -6 to 6
- left_env: float32 [4096, 24, 32, 32], P('sector', 'term'), may hold values from -1 to 1
- right_env: float32 [24, 128, 128], P('term'), may hold values from -0.5 to 0.5
- dest: int32 [4096, 8], P('sector', 'term'), may hold values from 0 to 4095, as said below
- block_rows: int32 [4096], P('sector'), may hold values from 1 to 32
Outputs:
- sigma: float32 [4096, 32, 128], P('sector', 'term')
Inputs may be any that keep to these rules, and one draw needn't show every extreme that they name: Block p belongs to index p // 64 of sector. Of the 64 * 8 // 8 pairs (q, g) that one device holds, at most 2 have dest on the blocks of one index of sector, and for every device exactly 2 do for some index.
All inputs are finite; a program needn't handle non-finite values.
Results may differ from a plain program's by a relative error of at most 0.0003.
Values sent between devices are 32-bit elements; how exact they have to be, the bound alone decides.
No kernel may reach another device: no remote copies, remote signals or barrier semaphores. Data moves between devices by JAX's collectives and lax.ppermute only.
A program may use at most 64 MiB of HBM per device.

v0:
```python
import jax
import jax.numpy as jnp
from jax import lax
from jax.sharding import PartitionSpec as P


def combine_slots(received, tags, blocks):
    select = (tags[None, :] == jnp.arange(blocks, dtype=jnp.float32)[:, None]).astype(jnp.float32)
    return jnp.dot(select, received, precision=lax.Precision.HIGHEST)


def per_device(psi, left_env, right_env, dest, block_rows):
    sectors = lax.axis_size("sector")
    blocks, groups = dest.shape
    channels = left_env.shape[1]
    share = channels // groups
    rows, cols = (psi.shape[1], psi.shape[2])
    slots = 2 * blocks * groups // sectors
    inner = jnp.einsum("qars,qsc->qarc", left_env, psi, precision=lax.Precision.HIGHEST)
    inner = inner.reshape(blocks, groups, share, rows, cols)
    rights = right_env.reshape(groups, share, cols, cols)
    summed = jnp.einsum("qgkrc,gkcd->qgrd", inner, rights, precision=lax.Precision.HIGHEST)
    items = summed.reshape(blocks * groups, rows, cols)
    target = dest.reshape(blocks * groups)
    owner = target // blocks
    local_block = target % blocks
    onehot = (owner[:, None] == jnp.arange(sectors, dtype=jnp.int32)[None, :]).astype(jnp.int32)
    slot = jnp.sum(jnp.cumsum(onehot, axis=0) * onehot, axis=1) - 1
    outbox = (
        jnp.zeros((sectors, slots, rows, cols), jnp.float32).at[owner, slot].set(items, mode="drop")
    )
    labels = (
        jnp.full((sectors, slots), -1.0, jnp.float32)
        .at[owner, slot]
        .set(local_block.astype(jnp.float32), mode="drop")
    )
    inbox, tags = (
        lax.all_to_all(outbox, "sector", split_axis=0, concat_axis=0, tiled=True),
        lax.all_to_all(labels, "sector", split_axis=0, concat_axis=0, tiled=True),
    )
    partial_value = combine_slots(inbox.reshape(-1, rows * cols), tags.reshape(-1), blocks).reshape(
        blocks, rows, cols
    )
    live = jnp.arange(rows, dtype=jnp.int32)[None, :] < block_rows[:, None]
    partial_value = jnp.where(live[:, :, None], partial_value, jnp.float32(0.0))
    return lax.psum_scatter(partial_value, "term", scatter_dimension=1, tiled=True)


def solution(mesh):
    in_specs = (
        P("sector", None, None),
        P("sector", "term", None, None),
        P("term", None, None),
        P("sector", "term"),
        P("sector"),
    )
    out_specs = P("sector", "term", None)
    return jax.shard_map(
        per_device, mesh=mesh, in_specs=in_specs, out_specs=out_specs, check_vma=False
    )
```

profile of v0, /device:TPU:2, one launch (start us, length us, event | category | flops | bytes accessed | tf_op | source)
XLA Modules:
  0.0 164.5 jit_solution(16468211979069713100)
XLA Ops:
  6.5 0.0 copy-start
  6.5 0.8 fusion.14
  7.3 0.7 fusion.8
  8.0 0.1 fusion.3
  8.0 0.1 reduce_window_sum.11
  8.1 0.2 select_reduce_fusion
  8.3 0.7 fusion.10
  9.0 3.5 %scatter_fusion = f32[64,2]{0,1:T(2,128)S(1)} fusion(f32[64,2]{0,1:T(2,128)S(1)} %broadcast_in_dim.13, s32[64]{0:T(128)S(1)} %fusion.10, f32[64]{0:T(128)S(1)} %fusion.8), kind=kCustom, calls=%fused_computation | custom fusion | bytes 1280 | tf_op jit(solution)/shard_map/scatter | solution.py:35
  12.5 0.7 copy.11
  13.2 13.9 %all-to-all-start = ((f32[64,1,2]{2,1,0:T(1,128)}), f32[64,1,2]{2,1,0:T(1,128)S(1)}, u32[]{:S(2)}, u32[]{:S(2)}) async-start(f32[64,1,2]{2,1,0:T(1,128)} %copy.11), calls=%async_computation | async-start | bytes 65536 | tf_op jit(solution)/shard_map/all_to_all | solution.py:39
  27.1 3.6 %copy.12 = f32[64,3,32,32]{3,2,1,0:T(8,128)} copy(f32[64,3,32,32]{0,3,2,1:T(8,128)} %param.6) | data formatting | bytes 1572864 | tf_op args[1]
  30.7 0.0 copy-done
  30.7 0.0 copy-start.1
  30.7 5.1 %fusion = f32[64,3,32,128]{3,2,1,0:T(8,128)S(1)} fusion(f32[64,3,32,32]{3,2,1,0:T(8,128)} %copy.12, f32[64,32,128]{2,1,0:T(8,128)S(1)} %copy-done), kind=kOutput, calls=%fused_computation.5 | convolution fusion | flops 301989888 | bytes 4980736 | tf_op jit(solution)/shard_map/qars,qsc->qarc/dot_general | solution.py:19
  35.8 0.0 copy-done.1
  35.8 3.0 %convolution_bitcast_fusion = f32[64,32,128]{2,1,0:T(8,128)S(1)} fusion(f32[64,3,32,128]{3,2,1,0:T(8,128)S(1)} %fusion, f32[3,128,128]{2,1,0:T(8,128)S(1)} %copy-done.1), kind=kOutput, calls=%fused_computation.4 | convolution fusion | flops 1207959552 | bytes 4390912 | tf_op jit(solution)/shard_map/qgkrc,gkcd->qgrd/dot_general | solution.py:22
  38.8 1.6 broadcast_in_dim.14
  40.4 8.9 %scatter_fusion.1 = f32[64,2,32,128]{3,2,1,0:T(8,128)} fusion(f32[64,2,32,128]{3,2,1,0:T(8,128)} %broadcast_in_dim.14, s32[64]{0:T(128)S(1)} %fusion.10, f32[64,32,128]{2,1,0:T(8,128)S(1)} %convolution_bitcast_fusion), kind=kCustom, calls=%fused_computation.1 | custom fusion | bytes 3146240 | tf_op jit(solution)/shard_map/scatter | solution.py:30
  49.3 0.0 copy-start.2
  49.3 0.0 all-to-all-done
  49.3 10.5 %all-to-all-start.1 = ((f32[64,2,32,128]{3,2,1,0:T(8,128)}), f32[64,2,32,128]{3,2,1,0:T(8,128)S(1)}, u32[]{:S(2)}, u32[]{:S(2)}) async-start(f32[64,2,32,128]{3,2,1,0:T(8,128)} %scatter_fusion.1), calls=%async_computation.1 | async-start | bytes 4194304 | tf_op jit(solution)/shard_map/all_to_all | solution.py:38
  59.8 0.2 reduce-scatter.2.cloned.1.call-start
  60.0 0.0 copy-done.2
  60.0 0.5 broadcast.127
  60.6 0.7 reduce.3
  61.3 0.1 eq.36
  61.4 47.9 %all-to-all-done.1 = f32[64,2,32,128]{3,2,1,0:T(8,128)S(1)} async-done(((f32[64,2,32,128]{3,2,1,0:T(8,128)}), f32[64,2,32,128]{3,2,1,0:T(8,128)S(1)}, u32[]{:S(2)}, u32[]{:S(2)}) %all-to-all-start.1) | async-done | bytes 2097184 | tf_op jit(solution)/shard_map/all_to_all | solution.py:38
  109.3 3.0 %copy.19 = f32[16,8,32,128]{3,1,2,0:T(8,128)} copy(f32[16,8,32,128]{3,2,1,0:T(8,128)S(1)} %bitcast.42) | data formatting | bytes 4194304
  112.3 1.9 %copy.13 = f32[4096,128]{1,0:T(8,128)S(1)} copy(f32[4096,128]{0,1:T(8,128)} %bitcast.44) | data formatting | bytes 4194304 | tf_op jit(solution)/shard_map/dot_general | solution.py:9
  114.2 2.3 %convolution_select_fusion = f32[64,32,128]{2,0,1:T(8,128)} fusion(f32[32,128,128]{2,1,0:T(8,128)S(1)} %bitcast.43, pred[64,32]{0,1:T(8,128)(4,1)S(1)} %iota_compare_fusion.2, f32[128]{0:T(128)S(1)} %eq.36), kind=kOutput, calls=%fused_computation.3 | convolution fusion | flops 402923520 | bytes 3148288 | tf_op jit(solution)/shard_map/dot_general | solution.py:9
  116.6 0.0 reduce-scatter.2.cloned.1.call-update
  116.6 39.5 %reduce-scatter.2.cloned.1.call-done = f32[64,4,128]{2,0,1:T(8,128)} async-done(((f32[64,32,128]{2,0,1:T(8,128)}), f32[64,4,128]{2,0,1:T(8,128)}) %reduce-scatter.2.cloned.1.call-update) | async-done | bytes 131088 | tf_op jit(solution)/shard_map/reduce_scatter | solution.py:46
  156.1 1.6 copy.14
  (2 shorter events, 0.0 us)
Async XLA Ops:
  6.5 24.2 %copy-start = (f32[64,32,128]{2,1,0:T(8,128)S(1)}, f32[64,32,128]{2,1,0:T(8,128)}, u32[]{:S(2)}) copy-start(f32[64,32,128]{2,1,0:T(8,128)} %param.5) | copy-start | bytes 3145732
  13.2 36.1 %all-to-all-start = ((f32[64,1,2]{2,1,0:T(1,128)}), f32[64,1,2]{2,1,0:T(1,128)S(1)}, u32[]{:S(2)}, u32[]{:S(2)}) async-start(f32[64,1,2]{2,1,0:T(1,128)} %copy.11), calls=%async_computation | async-start | bytes 65536 | tf_op jit(solution)/shard_map/all_to_all | solution.py:39
  30.7 5.1 %copy-start.1 = (f32[3,128,128]{2,1,0:T(8,128)S(1)}, f32[3,128,128]{2,1,0:T(8,128)}, u32[]{:S(2)}) copy-start(f32[3,128,128]{2,1,0:T(8,128)} %param.7) | copy-start | bytes 589828
  49.3 10.7 %copy-start.2 = (s32[64]{0:T(128)S(1)}, s32[64]{0:T(128)}, u32[]{:S(2)}) copy-start(s32[64]{0:T(128)} %param.9) | copy-start | bytes 772
  49.3 60.0 %all-to-all-start.1 = ((f32[64,2,32,128]{3,2,1,0:T(8,128)}), f32[64,2,32,128]{3,2,1,0:T(8,128)S(1)}, u32[]{:S(2)}, u32[]{:S(2)}) async-start(f32[64,2,32,128]{3,2,1,0:T(8,128)} %scatter_fusion.1), calls=%async_computation.1 | async-start | bytes 4194304 | tf_op jit(solution)/shard_map/all_to_all | solution.py:38
  59.8 96.3 %reduce-scatter.2.cloned.1.call-start = ((), (), s32[]{:S(2)}) async-start(), calls=%async_computation.3 | async-start | bytes 1179648 | tf_op jit(solution)/shard_map/reduce_scatter | solution.py:46
Sparse Core Ops, SparseCore 0:
  116.7 39.3 reduce-scatter.1
where the time goes:
time: 165 us
  waiting for transfers between devices  87.4 us (53%)
  local copies, waits for them, and re-layouts  25.5 us (15%)
  starting transfers between devices  24.6 us (15%)
  between operations  13.5 us (8%)
  matrix products  10.4 us (6%)
  other arithmetic  3.17 us (2%)
    all_to_all x1, waiting for transfers between devices, per_device(): lax.all_to_all(outbox, 'sector', split_axis=0, concat_axis=0, tiled=True)  47.9 us
    reduce_scatter x1, waiting for transfers between devices, per_device(): lax.psum_scatter(partial_value, 'term', scatter_dimension=1, tiled=True)  39.5 us
    all_to_all x1, starting transfers between devices, per_device(): lax.all_to_all(labels, 'sector', split_axis=0, concat_axis=0, tiled=True)  13.9 us
    all_to_all x1, starting transfers between devices, per_device(): lax.all_to_all(outbox, 'sector', split_axis=0, concat_axis=0, tiled=True)  10.5 us
    scatter x1, local copies, waits for them, and re-layouts, per_device(): jnp.zeros((sectors, slots, rows, cols), jnp.float32).at[owner, slot]  8.87 us
    unnamed x8, local copies, waits for them, and re-layouts  6.59 us
    dot_general x1, matrix products, per_device(): jnp.einsum('qars,qsc->qarc', left_env, psi, precision=lax.Precision.HIGHEST)  5.11 us
    scatter x1, local copies, waits for them, and re-layouts, per_device(): labels = jnp.full((sectors, slots), -1.0, jnp.float32).at[owner, slot].se...  3.5 us
  transfers between devices with their start and end apart: 3, of which 2 were waited for; matrix products, arithmetic and copies ran while one was open for 14% of the time, Pallas kernels for 0%

commit v1 on v0

v1 whole, which is shorter than its diff:
```python
import functools

import jax
import jax.numpy as jnp
from jax import lax
from jax.experimental import pallas as pl
from jax.experimental.pallas import tpu as pltpu
from jax.sharding import PartitionSpec as P

BF16, F32 = jnp.bfloat16, jnp.float32


def halves(x):
    high = x.astype(BF16)
    return high, (x - high.astype(F32)).astype(BF16)


def product_kernel(
    sectors, step, dest_ref, psi_ref, left_ref, right_ref, outbox_ref, marks_ref, rights, counts, inner
):
    blocks = dest_ref.shape[0]
    share, cols = right_ref.shape[0], right_ref.shape[1]
    rows = psi_ref.shape[1]
    pieces = outbox_ref.shape[0] // sectors
    depth = share * cols
    index = pl.program_id(0)

    @pl.when(index == 0)
    def begin():
        for k in range(share):
            high, low = halves(right_ref[k])
            rights[pl.ds(k * cols, cols), :cols] = high
            rights[pl.ds(k * cols, cols), cols:] = low
        outbox_ref[...] = jnp.zeros_like(outbox_ref)
        marks_ref[...] = jnp.zeros_like(marks_ref)

        def clear(owner, carry):
            counts[owner] = 0
            return carry

        lax.fori_loop(0, sectors, clear, 0)

    for b in range(step):
        left_high, left_low = halves(left_ref[b].reshape(share * rows, rows))
        psi_high, psi_low = halves(psi_ref[b])
        lefts = jnp.concatenate([left_high, left_low, left_high], axis=1)
        psis = jnp.concatenate([psi_high, psi_high, psi_low], axis=0)
        value = jnp.dot(lefts, psis, preferred_element_type=F32)
        for k in range(share):
            inner[pl.ds(b * rows, rows), k * cols : (k + 1) * cols] = value[k * rows : (k + 1) * rows]
    high, low = halves(inner[...])
    both = jnp.dot(high, rights[...], preferred_element_type=F32)
    items = both[:, :cols] + both[:, cols:]
    items = items + jnp.dot(low, rights[:, :cols], preferred_element_type=F32)

    place = lax.broadcasted_iota(jnp.int32, (8, cols), 0)
    lane = lax.broadcasted_iota(jnp.int32, (1, cols), 1)
    for b in range(step):
        target = dest_ref[index * step + b]
        owner, local = target // blocks, target % blocks
        slot = counts[owner]
        counts[owner] = slot + 1
        mine = (place // 4) == slot
        for v in range(rows // 8):
            whole = items[b * rows + v * 8 : b * rows + v * 8 + 8]
            turned = pltpu.roll(whole, 4, 0)
            even = jnp.where(slot == 0, whole, turned)
            odd = jnp.where(slot == 0, turned, whole)
            at = 2 * v * sectors + owner
            outbox_ref[at] = jnp.where(mine, even, outbox_ref[at])
            at = at + sectors
            outbox_ref[at] = jnp.where(mine, odd, outbox_ref[at])
        mark = (lane == slot * blocks + local).astype(F32)
        for piece in range(pieces):
            at = piece * sectors + owner
            marks_ref[at] = marks_ref[at] + mark


def products(dest, psi, left_env, right_env, sectors, terms):
    blocks, rows, cols = psi.shape
    share = right_env.shape[0]
    step = 16
    peers = sectors * terms
    return pl.pallas_call(
        functools.partial(product_kernel, sectors, step),
        grid=(blocks // step,),
        in_specs=[
            pl.BlockSpec(memory_space=pltpu.SMEM),
            pl.BlockSpec((step, rows, cols), lambda i: (i, 0, 0)),
            pl.BlockSpec((step, share, rows, rows), lambda i: (i, 0, 0, 0)),
            pl.BlockSpec((share, cols, cols), lambda i: (0, 0, 0)),
        ],
        out_specs=[
            pl.BlockSpec((peers, 8, cols), lambda i: (0, 0, 0)),
            pl.BlockSpec((peers, 1, cols), lambda i: (0, 0, 0)),
        ],
        out_shape=[
            jax.ShapeDtypeStruct((peers, 8, cols), F32),
            jax.ShapeDtypeStruct((peers, 1, cols), F32),
        ],
        scratch_shapes=[
            pltpu.VMEM((share * cols, 2 * cols), BF16),
            pltpu.SMEM((sectors,), jnp.int32),
            pltpu.VMEM((step * rows, share * cols), F32),
        ],
        compiler_params=pltpu.CompilerParams(vmem_limit_bytes=40 * 1024 * 1024),
    )(dest, psi, left_env, right_env)


def combine_kernel(term_ref, inbox_ref, marks_ref, live_ref, out_ref, total):
    index = pl.program_id(0)
    sources, rows2, cols = inbox_ref.shape
    blocks, rows = out_ref.shape[0], out_ref.shape[1]

    @pl.when(index == 0)
    def begin():
        total[...] = jnp.zeros_like(total)

    marks = marks_ref[...].reshape(sources, cols).astype(BF16)
    for slot in range(rows2 // rows):
        got = jnp.concatenate([inbox_ref[:, slot * rows + r, :] for r in range(rows)], axis=1)
        high, low = halves(got)
        select = marks[:, slot * blocks : (slot + 1) * blocks]
        dims = (((0,), (0,)), ((), ()))
        total[...] += lax.dot_general(select, high, dims, preferred_element_type=F32)
        total[...] += lax.dot_general(select, low, dims, preferred_element_type=F32)

    @pl.when(index == pl.num_programs(0) - 1)
    def end():
        for r in range(rows):
            alive = term_ref[0] * rows + r < live_ref[...]
            out_ref[:, r, :] = jnp.where(alive, total[:, r * cols : (r + 1) * cols], 0.0)


def combine(term, inbox, marks, block_rows, rows):
    peers, rows2, cols = inbox.shape
    blocks = block_rows.shape[0]
    step = 128
    return pl.pallas_call(
        combine_kernel,
        grid=(peers // step,),
        in_specs=[
            pl.BlockSpec(memory_space=pltpu.SMEM),
            pl.BlockSpec((step, rows2, cols), lambda i: (i, 0, 0)),
            pl.BlockSpec((step, 1, cols), lambda i: (i, 0, 0)),
            pl.BlockSpec((blocks, 1), lambda i: (0, 0)),
        ],
        out_specs=pl.BlockSpec((blocks, rows, cols), lambda i: (0, 0, 0)),
        out_shape=jax.ShapeDtypeStruct((blocks, rows, cols), F32),
        scratch_shapes=[pltpu.VMEM((blocks, rows * cols), F32)],
        compiler_params=pltpu.CompilerParams(vmem_limit_bytes=40 * 1024 * 1024),
    )(term, inbox, marks, block_rows.reshape(blocks, 1))


def per_device(psi, left_env, right_env, dest, block_rows):
    sectors, terms = lax.axis_size("sector"), lax.axis_size("term")
    rows = psi.shape[1] // terms
    outbox, marks = products(dest.reshape(-1), psi, left_env, right_env, sectors, terms)
    everyone = ("term", "sector")
    inbox = lax.all_to_all(outbox, everyone, split_axis=0, concat_axis=0, tiled=True)
    got_marks = lax.all_to_all(marks, everyone, split_axis=0, concat_axis=0, tiled=True)
    term = lax.axis_index("term").reshape(1)
    return combine(term, inbox, got_marks, block_rows, rows)


def solution(mesh):
    in_specs = (
        P("sector", None, None),
        P("sector", "term", None, None),
        P("term", None, None),
        P("sector", "term"),
        P("sector"),
    )
    out_specs = P("sector", "term", None)
    return jax.shard_map(
        per_device, mesh=mesh, in_specs=in_specs, out_specs=out_specs, check_vma=False
    )
```

time: 165 us -> 115 us (0.70)
  the two profiles are of different devices: /device:TPU:2 before, /device:TPU:1 now
where the time goes in v1:
time: 115 us
  waiting for transfers between devices  55.1 us (48%)
  blocking collectives  39.3 us (34%)
  starting transfers between devices  8.67 us (8%)
  Pallas kernels  7.53 us (7%)
  local copies, waits for them, and re-layouts  4.2 us (4%)
    all_to_all x1, waiting for transfers between devices, per_device(): lax.all_to_all(outbox, everyone, split_axis=0, concat_axis=0, tiled=True)  55.1 us
    all_to_all x1, blocking collectives, per_device(): lax.all_to_all(marks, everyone, split_axis=0, concat_axis=0, tiled=True)  39.3 us
    all_to_all x1, starting transfers between devices, per_device(): lax.all_to_all(outbox, everyone, split_axis=0, concat_axis=0, tiled=True)  8.67 us
    pallas_call x1, Pallas kernels, products(): pl.pallas_call(functools.partial(product_kernel, sectors, step), grid=(bl...  4.54 us
    unnamed x11, local copies, waits for them, and re-layouts  4.11 us
    pallas_call x1, Pallas kernels, combine(): pl.pallas_call(combine_kernel, grid=(peers // step,), in_specs=[pl.BlockS...  2.99 us
  transfers between devices with their start and end apart: 1, of which 1 were waited for; matrix products, arithmetic and copies ran while one was open for 0% of the time, Pallas kernels for 0%

profile of v1, /device:TPU:1, one launch (start us, length us, event | category | flops | bytes accessed | tf_op | source)
XLA Modules:
  0.0 115.0 jit_solution(11729067253436586493)
XLA Ops:
  0.0 0.0 copy-start.3
  0.0 0.0 copy-start.2
  0.0 2.9 %copy.6.left_ref = f32[64,3,32,32]{3,2,1,0:T(8,128)S(1)} copy(f32[64,3,32,32]{0,3,2,1:T(8,128)} %param.6) | data formatting | bytes 1572864 | tf_op args[1]
  2.9 0.0 copy-done.3
  2.9 0.0 copy-done.2
  2.9 0.0 copy-start.1
  2.9 1.2 %copy-done.1 = f32[64,32,128]{2,1,0:T(8,128)S(1)} copy-done((f32[64,32,128]{2,1,0:T(8,128)S(1)}, f32[64,32,128]{2,1,0:T(8,128)}, u32[]{:S(2)}) %copy-start.1) | copy-done | bytes 1048600
  4.1 4.5 %shard_map.55 = (f32[512,8,128]{2,1,0:T(8,128)S(1)}, f32[512,1,128]{2,1,0:T(1,128)S(1)}) custom-call(s32[64]{0:T(128)S(1)} %bitcast.3, f32[64,32,128]{2,1,0:T(8,128)S(1)} %copy-done.1, f32[64,3,32,32]{3,2,1,0:T(8,128)S(1)} %copy.6.left_ref, f32[3,128,128]{2,1,0:T(8,128)S(1)} %copy-done.2), custom_call_target="tpu_custom_call" | custom-call | tf_op jit(solution)/shard_map/pallas_call | solution.py:84
  8.7 0.0 copy-start
  8.7 39.3 %all_to_all.10.marks_ref = f32[512,1,128]{2,1,0:T(1,128)S(1)} all-to-all(f32[512,1,128]{2,1,0:T(1,128)S(1)} %get-tuple-element.8), channel_id=1, replica_groups=mesh['term'=8,'sector'=64] {'term','sector'}, dimensions={0} | all-to-all | bytes 524288 | tf_op jit(solution)/shard_map/all_to_all | solution.py:161
  48.0 0.0 copy-done
  48.0 0.0 copy-start.4
  48.0 8.7 %all-to-all-start = ((f32[512,8,128]{2,1,0:T(8,128)}), f32[512,8,128]{2,1,0:T(8,128)S(1)}, u32[]{:S(2)}, u32[]{:S(2)}) async-start(f32[512,8,128]{2,1,0:T(8,128)} %copy-done), calls=%async_computation | async-start | bytes 4194304 | tf_op jit(solution)/shard_map/all_to_all | solution.py:160
  56.7 0.0 copy-done.4
  56.7 0.1 copy.7.live_ref
  56.8 55.1 %all-to-all-done.inbox_ref = f32[512,8,128]{2,1,0:T(8,128)S(1)} async-done(((f32[512,8,128]{2,1,0:T(8,128)}), f32[512,8,128]{2,1,0:T(8,128)S(1)}, u32[]{:S(2)}, u32[]{:S(2)}) %all-to-all-start) | async-done | bytes 2097184 | tf_op jit(solution)/shard_map/all_to_all | solution.py:160
  112.0 3.0 %shard_map.56 = f32[64,4,128]{2,1,0:T(4,128)} custom-call(s32[1]{0:T(128)} %bitcast.term_ref, f32[512,8,128]{2,1,0:T(8,128)S(1)} %all-to-all-done.inbox_ref, f32[512,1,128]{2,1,0:T(1,128)S(1)} %all_to_all.10.marks_ref, s32[64,1]{1,0:T(8,128)S(1)} %copy.7.live_ref), custom_call_target="tpu_custom_call" | custom-call | tf_op jit(solution)/shard_map/pallas_call | solution.py:139
Async XLA Ops:
  0.0 2.9 %copy-start.3 = (s32[64,1]{0,1:T(1,128)S(1)}, s32[64,1]{0,1:T(1,128)}, u32[]{:S(2)}) copy-start(s32[64,1]{0,1:T(1,128)} %param.8) | copy-start | bytes 772
  0.0 2.9 %copy-start.2 = (f32[3,128,128]{2,1,0:T(8,128)S(1)}, f32[3,128,128]{2,1,0:T(8,128)}, u32[]{:S(2)}) copy-start(f32[3,128,128]{2,1,0:T(8,128)} %right_ref.1) | copy-start | bytes 589828
  2.9 1.2 %copy-start.1 = (f32[64,32,128]{2,1,0:T(8,128)S(1)}, f32[64,32,128]{2,1,0:T(8,128)}, u32[]{:S(2)}) copy-start(f32[64,32,128]{2,1,0:T(8,128)} %psi_ref.1) | copy-start | bytes 3145732
  8.7 39.4 %copy-start = (f32[512,8,128]{2,1,0:T(8,128)}, f32[512,8,128]{2,1,0:T(8,128)S(1)}, u32[]{:S(2)}) copy-start(f32[512,8,128]{2,1,0:T(8,128)S(1)} %get-tuple-element.7) | copy-start | bytes 6291460
  48.0 8.7 %copy-start.4 = (s32[64]{0:T(128)S(1)}, s32[64]{0:T(128)}, u32[]{:S(2)}) copy-start(s32[64]{0:T(128)} %param.9) | copy-start | bytes 772
  48.0 63.9 %all-to-all-start = ((f32[512,8,128]{2,1,0:T(8,128)}), f32[512,8,128]{2,1,0:T(8,128)S(1)}, u32[]{:S(2)}, u32[]{:S(2)}) async-start(f32[512,8,128]{2,1,0:T(8,128)} %copy-done), calls=%async_computation | async-start | bytes 4194304 | tf_op jit(solution)/shard_map/all_to_all | solution.py:160

commit v2 on v1

v2 whole, which is shorter than its diff:
```python
import functools

import jax
import jax.numpy as jnp
from jax import lax
from jax.experimental import pallas as pl
from jax.experimental.pallas import tpu as pltpu
from jax.sharding import PartitionSpec as P

BF16, F32 = jnp.bfloat16, jnp.float32


def halves(x):
    high = x.astype(BF16)
    return high, (x - high.astype(F32)).astype(BF16)


def product_kernel(
    sectors, step, dest_ref, psi_ref, left_ref, right_ref, outbox_ref, rights, counts, inner
):
    blocks = dest_ref.shape[0]
    share, cols = right_ref.shape[0], right_ref.shape[1]
    rows = psi_ref.shape[1]
    pieces = outbox_ref.shape[0] // sectors
    held = rows // pieces
    index = pl.program_id(0)

    @pl.when(index == 0)
    def begin():
        for k in range(share):
            high, low = halves(right_ref[k])
            rights[pl.ds(k * cols, cols), :cols] = high
            rights[pl.ds(k * cols, cols), cols:] = low
        outbox_ref[...] = jnp.zeros_like(outbox_ref)

        def clear(owner, carry):
            counts[owner] = 0
            return carry

        lax.fori_loop(0, sectors, clear, 0)

    for b in range(step):
        left_high, left_low = halves(left_ref[b].reshape(share * rows, rows))
        psi_high, psi_low = halves(psi_ref[b])
        lefts = jnp.concatenate([left_high, left_low, left_high], axis=1)
        psis = jnp.concatenate([psi_high, psi_high, psi_low], axis=0)
        value = jnp.dot(lefts, psis, preferred_element_type=F32)
        for k in range(share):
            inner[pl.ds(b * rows, rows), k * cols : (k + 1) * cols] = value[k * rows : (k + 1) * rows]
    high, low = halves(inner[...])
    both = jnp.dot(high, rights[...], preferred_element_type=F32)
    items = both[:, :cols] + both[:, cols:]
    items = items + jnp.dot(low, rights[:, :cols], preferred_element_type=F32)

    lane = lax.broadcasted_iota(jnp.int32, (1, cols), 1)
    for b in range(step):
        target = dest_ref[index * step + b]
        owner, local = target // blocks, target % blocks
        slot = counts[owner]
        counts[owner] = slot + 1
        mark = (lane == slot * blocks + local).astype(F32)
        for piece in range(pieces):
            at = piece * sectors + owner
            for r in range(held):
                row = b * rows + piece * held + r
                outbox_ref[at, slot * held + r] = items[row : row + 1]
            outbox_ref[at, 2 * held] = outbox_ref[at, 2 * held] + mark


def products(dest, psi, left_env, right_env, sectors, terms):
    blocks, rows, cols = psi.shape
    share = right_env.shape[0]
    step = 16
    peers = sectors * terms
    message = 2 * (rows // terms) + 1
    return pl.pallas_call(
        functools.partial(product_kernel, sectors, step),
        grid=(blocks // step,),
        in_specs=[
            pl.BlockSpec(memory_space=pltpu.SMEM),
            pl.BlockSpec((step, rows, cols), lambda i: (i, 0, 0)),
            pl.BlockSpec((step, share, rows, rows), lambda i: (i, 0, 0, 0)),
            pl.BlockSpec((share, cols, cols), lambda i: (0, 0, 0)),
        ],
        out_specs=pl.BlockSpec((peers, message, 1, cols), lambda i: (0, 0, 0, 0)),
        out_shape=jax.ShapeDtypeStruct((peers, message, 1, cols), F32),
        scratch_shapes=[
            pltpu.VMEM((share * cols, 2 * cols), BF16),
            pltpu.SMEM((sectors,), jnp.int32),
            pltpu.VMEM((step * rows, share * cols), F32),
        ],
        compiler_params=pltpu.CompilerParams(vmem_limit_bytes=40 * 1024 * 1024),
    )(dest, psi, left_env, right_env)


def combine_kernel(term_ref, inbox_ref, live_ref, out_ref, total):
    index = pl.program_id(0)
    cols = inbox_ref.shape[-1]
    blocks, rows = out_ref.shape[0], out_ref.shape[1]

    @pl.when(index == 0)
    def begin():
        total[...] = jnp.zeros_like(total)

    marks = inbox_ref[:, 2 * rows, 0, :].astype(BF16)
    for slot in range(2):
        got = jnp.concatenate([inbox_ref[:, slot * rows + r, 0, :] for r in range(rows)], axis=1)
        high, low = halves(got)
        select = marks[:, slot * blocks : (slot + 1) * blocks]
        dims = (((0,), (0,)), ((), ()))
        total[...] += lax.dot_general(select, high, dims, preferred_element_type=F32)
        total[...] += lax.dot_general(select, low, dims, preferred_element_type=F32)

    @pl.when(index == pl.num_programs(0) - 1)
    def end():
        for r in range(rows):
            alive = term_ref[0] * rows + r < live_ref[...]
            out_ref[:, r, :] = jnp.where(alive, total[:, r * cols : (r + 1) * cols], 0.0)


def combine(term, inbox, block_rows, rows):
    peers, message, _, cols = inbox.shape
    blocks = block_rows.shape[0]
    step = 128
    return pl.pallas_call(
        combine_kernel,
        grid=(peers // step,),
        in_specs=[
            pl.BlockSpec(memory_space=pltpu.SMEM),
            pl.BlockSpec((step, message, 1, cols), lambda i: (i, 0, 0, 0)),
            pl.BlockSpec((blocks, 1), lambda i: (0, 0)),
        ],
        out_specs=pl.BlockSpec((blocks, rows, cols), lambda i: (0, 0, 0)),
        out_shape=jax.ShapeDtypeStruct((blocks, rows, cols), F32),
        scratch_shapes=[pltpu.VMEM((blocks, rows * cols), F32)],
        compiler_params=pltpu.CompilerParams(vmem_limit_bytes=40 * 1024 * 1024),
    )(term, inbox, block_rows.reshape(blocks, 1))


def per_device(psi, left_env, right_env, dest, block_rows):
    sectors, terms = lax.axis_size("sector"), lax.axis_size("term")
    rows = psi.shape[1] // terms
    outbox = products(dest.reshape(-1), psi, left_env, right_env, sectors, terms)
    everyone = ("term", "sector")
    inbox = lax.all_to_all(outbox, everyone, split_axis=0, concat_axis=0, tiled=True)
    term = lax.axis_index("term").reshape(1)
    return combine(term, inbox, block_rows, rows)


def solution(mesh):
    in_specs = (
        P("sector", None, None),
        P("sector", "term", None, None),
        P("term", None, None),
        P("sector", "term"),
        P("sector"),
    )
    out_specs = P("sector", "term", None)
    return jax.shard_map(
        per_device, mesh=mesh, in_specs=in_specs, out_specs=out_specs, check_vma=False
    )
```

time: 115 us -> 97.5 us (0.85)
  blocking collectives: 39.3 us -> 0 us
  starting transfers between devices: 8.67 us -> 22.2 us
  waiting for transfers between devices: 55.1 us -> 60.4 us
  Pallas kernels: 7.53 us -> 9.15 us
  local copies, waits for them, and re-layouts: 4.2 us -> 5.47 us
    all_to_all x1 -> x0, blocking collectives: 39.3 us -> none  [per_device(): lax.all_to_all(marks, everyone, split_axis=0, concat_axis=0, tiled=True)]
    all_to_all x1, starting transfers between devices: 8.67 us -> 22.2 us  [per_device(): lax.all_to_all(outbox, everyone, split_axis=0, concat_axis=0, tiled=True)]
    all_to_all x1, waiting for transfers between devices: 55.1 us -> 60.4 us  [per_device(): lax.all_to_all(outbox, everyone, split_axis=0, concat_axis=0, tiled=True)]
    pallas_call x1, Pallas kernels: 4.54 us -> 6.43 us  [products(): pl.pallas_call(functools.partial(product_kernel, sectors, step), grid=(bl...]
    unnamed x11, local copies, waits for them, and re-layouts: 4.11 us -> 5.37 us
where the time goes in v2:
time: 97.5 us; the launch traced here: 97.3 us
  waiting for transfers between devices  60.4 us (62%)
  starting transfers between devices  22.2 us (23%)
  Pallas kernels  9.15 us (9%)
  local copies, waits for them, and re-layouts  5.47 us (6%)
    all_to_all x1, waiting for transfers between devices, per_device(): lax.all_to_all(outbox, everyone, split_axis=0, concat_axis=0, tiled=True)  60.4 us
    all_to_all x1, starting transfers between devices, per_device(): lax.all_to_all(outbox, everyone, split_axis=0, concat_axis=0, tiled=True)  22.2 us
    pallas_call x1, Pallas kernels, products(): pl.pallas_call(functools.partial(product_kernel, sectors, step), grid=(bl...  6.43 us
    unnamed x11, local copies, waits for them, and re-layouts  5.37 us
    pallas_call x1, Pallas kernels, combine(): pl.pallas_call(combine_kernel, grid=(peers // step,), in_specs=[pl.BlockS...  2.72 us
  transfers between devices with their start and end apart: 1, of which 1 were waited for; matrix products, arithmetic and copies ran while one was open for 0% of the time, Pallas kernels for 0%

profile of v2, /device:TPU:1, one launch (start us, length us, event | category | flops | bytes accessed | tf_op | source)
XLA Modules:
  0.0 97.3 jit_solution(3657276041079587146)
XLA Ops:
  0.0 0.0 copy-start.3
  0.0 0.0 copy-start.2
  0.0 2.7 %copy.6.left_ref = f32[64,3,32,32]{3,2,1,0:T(8,128)S(1)} copy(f32[64,3,32,32]{0,3,2,1:T(8,128)} %param.6) | data formatting | bytes 1572864 | tf_op args[1]
  2.8 0.0 copy-done.3
  2.8 0.0 copy-done.2
  2.8 0.0 copy-start.1
  2.8 1.2 %copy-done.1 = f32[64,32,128]{2,1,0:T(8,128)S(1)} copy-done((f32[64,32,128]{2,1,0:T(8,128)S(1)}, f32[64,32,128]{2,1,0:T(8,128)}, u32[]{:S(2)}) %copy-start.1) | copy-done | bytes 1048600
  4.0 6.4 %shard_map.55 = f32[512,9,1,128]{3,2,1,0:T(1,128)S(1)} custom-call(s32[64]{0:T(128)S(1)} %bitcast.3, f32[64,32,128]{2,1,0:T(8,128)S(1)} %copy-done.1, f32[64,3,32,32]{3,2,1,0:T(8,128)S(1)} %copy.6.left_ref, f32[3,128,128]{2,1,0:T(8,128)S(1)} %copy-done.2), custom_call_target="tpu_custom_call" | custom-call | tf_op jit(solution)/shard_map/pallas_call | solution.py:76
  10.4 0.0 copy-start
  10.4 1.4 %copy-done = f32[512,9,1,128]{3,2,1,0:T(1,128)} copy-done((f32[512,9,1,128]{3,2,1,0:T(1,128)}, f32[512,9,1,128]{3,2,1,0:T(1,128)S(1)}, u32[]{:S(2)}) %copy-start) | copy-done | bytes 2359320
  11.8 0.0 copy-start.4
  11.9 22.2 %all-to-all-start = ((f32[512,9,1,128]{3,2,1,0:T(1,128)}), f32[512,9,1,128]{3,2,1,0:T(1,128)S(1)}, u32[]{:S(2)}, u32[]{:S(2)}) async-start(f32[512,9,1,128]{3,2,1,0:T(1,128)} %copy-done), calls=%async_computation | async-start | bytes 4718592 | tf_op jit(solution)/shard_map/all_to_all | solution.py:145
  34.0 0.0 copy-done.4
  34.0 0.1 copy.7.live_ref
  34.1 60.4 %all-to-all-done.inbox_ref = f32[512,9,1,128]{3,2,1,0:T(1,128)S(1)} async-done(((f32[512,9,1,128]{3,2,1,0:T(1,128)}), f32[512,9,1,128]{3,2,1,0:T(1,128)S(1)}, u32[]{:S(2)}, u32[]{:S(2)}) %all-to-all-start) | async-done | bytes 2359328 | tf_op jit(solution)/shard_map/all_to_all | solution.py:145
  94.5 2.7 %shard_map.56 = f32[64,4,128]{2,1,0:T(4,128)} custom-call(s32[1]{0:T(128)} %bitcast.term_ref, f32[512,9,1,128]{3,2,1,0:T(1,128)S(1)} %all-to-all-done.inbox_ref, s32[64,1]{1,0:T(8,128)S(1)} %copy.7.live_ref), custom_call_target="tpu_custom_call" | custom-call | tf_op jit(solution)/shard_map/pallas_call | solution.py:125
Async XLA Ops:
  0.0 2.8 %copy-start.3 = (s32[64,1]{0,1:T(1,128)S(1)}, s32[64,1]{0,1:T(1,128)}, u32[]{:S(2)}) copy-start(s32[64,1]{0,1:T(1,128)} %param.8) | copy-start | bytes 772
  0.0 2.8 %copy-start.2 = (f32[3,128,128]{2,1,0:T(8,128)S(1)}, f32[3,128,128]{2,1,0:T(8,128)}, u32[]{:S(2)}) copy-start(f32[3,128,128]{2,1,0:T(8,128)} %right_ref.1) | copy-start | bytes 589828
  2.8 1.2 %copy-start.1 = (f32[64,32,128]{2,1,0:T(8,128)S(1)}, f32[64,32,128]{2,1,0:T(8,128)}, u32[]{:S(2)}) copy-start(f32[64,32,128]{2,1,0:T(8,128)} %psi_ref.1) | copy-start | bytes 3145732
  10.4 1.4 %copy-start = (f32[512,9,1,128]{3,2,1,0:T(1,128)}, f32[512,9,1,128]{3,2,1,0:T(1,128)S(1)}, u32[]{:S(2)}) copy-start(f32[512,9,1,128]{3,2,1,0:T(1,128)S(1)} %shard_map.55) | copy-start | bytes 7077892
  11.8 22.2 %copy-start.4 = (s32[64]{0:T(128)S(1)}, s32[64]{0:T(128)}, u32[]{:S(2)}) copy-start(s32[64]{0:T(128)} %param.9) | copy-start | bytes 772
  11.9 82.7 %all-to-all-start = ((f32[512,9,1,128]{3,2,1,0:T(1,128)}), f32[512,9,1,128]{3,2,1,0:T(1,128)S(1)}, u32[]{:S(2)}, u32[]{:S(2)}) async-start(f32[512,9,1,128]{3,2,1,0:T(1,128)} %copy-done), calls=%async_computation | async-start | bytes 4718592 | tf_op jit(solution)/shard_map/all_to_all | solution.py:145

commit v3 on v2

v3 whole, which is shorter than its diff:
```python
import functools

import jax
import jax.numpy as jnp
from jax import lax
from jax.experimental import pallas as pl
from jax.experimental.pallas import tpu as pltpu
from jax.sharding import PartitionSpec as P

BF16, F32 = jnp.bfloat16, jnp.float32


def halves(x):
    high = x.astype(BF16)
    return high, (x - high.astype(F32)).astype(BF16)


def product_kernel(
    sectors, terms, step,
    dest_ref, psi_hbm, left_hbm, right_hbm, out_hbm,
    psi, left, right, turned, rights, counts, inner, outbox, marks, sems,
):
    blocks, rows, cols = psi.shape
    share = right.shape[0]
    held = rows // terms
    message = 2 * held + 1
    pack = cols // rows
    groups = share * rows // pack

    fetches = [
        pltpu.make_async_copy(left_hbm, left, sems.at[0]),
        pltpu.make_async_copy(right_hbm, right, sems.at[1]),
        pltpu.make_async_copy(psi_hbm, psi, sems.at[2]),
    ]
    for fetch in fetches:
        fetch.start()

    outbox[...] = jnp.zeros_like(outbox)
    marks[...] = jnp.zeros_like(marks)

    def clear(owner, carry):
        counts[owner] = 0
        return carry

    lax.fori_loop(0, sectors, clear, 0)

    fetches[0].wait()
    for g in range(groups):
        slabs = []
        for j in range(pack):
            at = j * groups + g
            slabs.append(left[at // rows, at % rows])
        slab = jnp.concatenate(slabs, axis=0)
        turned[g * blocks : (g + 1) * blocks, :] = slab.T
    fetches[1].wait()
    for k in range(share):
        high, low = halves(right[k])
        rights[k * cols : (k + 1) * cols, :cols] = high
        rights[k * cols : (k + 1) * cols, cols:] = low
    fetches[2].wait()

    lane = lax.broadcasted_iota(jnp.int32, (1, cols), 1)
    wide = lax.broadcasted_iota(jnp.int32, (groups, cols), 1)
    front, even = wide < cols // 2, (wide // rows) % 2 == 0

    def chunk(index, carry):
        for b in range(step):
            q = index * step + b
            mine = turned[pl.ds(q, groups, stride=blocks), :]
            high = mine.astype(BF16).astype(F32)
            low = mine - high
            highs = [high] + [pltpu.roll(high, rows * m, 1) for m in range(1, pack)]
            lows = [low] + [pltpu.roll(low, rows * m, 1) for m in range(1, pack)]
            parts = []
            for j in range(pack):
                h = jnp.where(front, highs[-j % pack], highs[(2 - j) % pack])
                l = jnp.where(front, lows[(1 - j) % pack], lows[(3 - j) % pack])
                parts.append(jnp.where(even, h, l))
            lefts = jnp.concatenate(parts, axis=0).astype(BF16)
            psi_high, psi_low = halves(psi[q])
            psis = jnp.concatenate([psi_high, psi_high, psi_low, psi_low], axis=0)
            value = jnp.dot(lefts, psis, preferred_element_type=F32)
            for k in range(share):
                inner[b * rows : (b + 1) * rows, k * cols : (k + 1) * cols] = value[k * rows : (k + 1) * rows]
        high, low = halves(inner[...])
        both = jnp.dot(high, rights[...], preferred_element_type=F32)
        items = both[:, :cols] + both[:, cols:]
        items = items + jnp.dot(low, rights[:, :cols], preferred_element_type=F32)
        for b in range(step):
            target = dest_ref[index * step + b]
            owner, local = target // blocks, target % blocks
            slot = counts[owner]
            counts[owner] = slot + 1
            marks[pl.ds(owner, 1), :] += (lane == slot * blocks + local).astype(F32)
            base = owner * message + slot * held
            for piece in range(terms):
                row = b * rows + piece * held
                outbox[pl.ds(base + piece * sectors * message, held), :] = items[row : row + held]
        return carry

    lax.fori_loop(0, blocks // step, chunk, 0)
    for piece in range(terms):
        at = piece * sectors * message + 2 * held
        outbox[pl.ds(at, sectors, stride=message), :] = marks[...]
    push = pltpu.make_async_copy(outbox, out_hbm, sems.at[0])
    push.start()
    push.wait()


def products(dest, psi, left_env, right_env, sectors, terms):
    blocks, rows, cols = psi.shape
    share = right_env.shape[0]
    step = 16
    message = 2 * (rows // terms) + 1
    total = sectors * terms * message
    hbm = pl.BlockSpec(memory_space=pltpu.HBM)
    out = pl.pallas_call(
        functools.partial(product_kernel, sectors, terms, step),
        in_specs=[pl.BlockSpec(memory_space=pltpu.SMEM), hbm, hbm, hbm],
        out_specs=hbm,
        out_shape=jax.ShapeDtypeStruct((total, cols), F32),
        scratch_shapes=[
            pltpu.VMEM((blocks, rows, cols), F32),
            pltpu.VMEM((share, rows, rows, blocks), F32),
            pltpu.VMEM((share, cols, cols), F32),
            pltpu.VMEM((share * rows * rows * blocks // cols, cols), F32),
            pltpu.VMEM((share * cols, 2 * cols), BF16),
            pltpu.SMEM((sectors,), jnp.int32),
            pltpu.VMEM((step * rows, share * cols), F32),
            pltpu.VMEM((total, cols), F32),
            pltpu.VMEM((sectors, cols), F32),
            pltpu.SemaphoreType.DMA((3,)),
        ],
        compiler_params=pltpu.CompilerParams(vmem_limit_bytes=60 * 1024 * 1024),
    )(dest, psi, jnp.transpose(left_env, (1, 2, 3, 0)), right_env)
    return out.reshape(sectors * terms, message, 1, cols)


def combine_kernel(term_ref, inbox_ref, live_ref, out_ref, total):
    index = pl.program_id(0)
    cols = inbox_ref.shape[-1]
    blocks, rows = out_ref.shape[0], out_ref.shape[1]

    @pl.when(index == 0)
    def begin():
        total[...] = jnp.zeros_like(total)

    marks = inbox_ref[:, 2 * rows, 0, :].astype(BF16)
    for slot in range(2):
        got = jnp.concatenate([inbox_ref[:, slot * rows + r, 0, :] for r in range(rows)], axis=1)
        high, low = halves(got)
        select = marks[:, slot * blocks : (slot + 1) * blocks]
        dims = (((0,), (0,)), ((), ()))
        total[...] += lax.dot_general(select, high, dims, preferred_element_type=F32)
        total[...] += lax.dot_general(select, low, dims, preferred_element_type=F32)

    @pl.when(index == pl.num_programs(0) - 1)
    def end():
        for r in range(rows):
            alive = term_ref[0] * rows + r < live_ref[...]
            out_ref[:, r, :] = jnp.where(alive, total[:, r * cols : (r + 1) * cols], 0.0)


def combine(term, inbox, block_rows, rows):
    peers, message, _, cols = inbox.shape
    blocks = block_rows.shape[0]
    step = 128
    return pl.pallas_call(
        combine_kernel,
        grid=(peers // step,),
        in_specs=[
            pl.BlockSpec(memory_space=pltpu.SMEM),
            pl.BlockSpec((step, message, 1, cols), lambda i: (i, 0, 0, 0)),
            pl.BlockSpec((blocks, 1), lambda i: (0, 0)),
        ],
        out_specs=pl.BlockSpec((blocks, rows, cols), lambda i: (0, 0, 0)),
        out_shape=jax.ShapeDtypeStruct((blocks, rows, cols), F32),
        scratch_shapes=[pltpu.VMEM((blocks, rows * cols), F32)],
        compiler_params=pltpu.CompilerParams(vmem_limit_bytes=40 * 1024 * 1024),
    )(term, inbox, block_rows.reshape(blocks, 1))


def per_device(psi, left_env, right_env, dest, block_rows):
    sectors, terms = lax.axis_size("sector"), lax.axis_size("term")
    rows = psi.shape[1] // terms
    outbox = products(dest.reshape(-1), psi, left_env, right_env, sectors, terms)
    inbox = lax.all_to_all(outbox, ("term", "sector"), split_axis=0, concat_axis=0, tiled=True)
    term = lax.axis_index("term").reshape(1)
    return combine(term, inbox, block_rows, rows)


def solution(mesh):
    in_specs = (
        P("sector", None, None),
        P("sector", "term", None, None),
        P("term", None, None),
        P("sector", "term"),
        P("sector"),
    )
    out_specs = P("sector", "term", None)
    return jax.shard_map(
        per_device, mesh=mesh, in_specs=in_specs, out_specs=out_specs, check_vma=False
    )
```

time: 97.5 us -> 92.8 us (0.952)
  local copies, waits for them, and re-layouts: 5.47 us -> 0.1 us
    unnamed x11 -> x2, local copies, waits for them, and re-layouts: 5.37 us -> 0.01 us
where the time goes in v3:
time: 92.8 us; the launch traced here: 92.6 us
  waiting for transfers between devices  60.4 us (65%)
  starting transfers between devices  22.2 us (24%)
  Pallas kernels  9.91 us (11%)
    all_to_all x1, waiting for transfers between devices, per_device(): lax.all_to_all(outbox, ('term', 'sector'), split_axis=0, concat_axis=0, t...  60.4 us
    all_to_all x1, starting transfers between devices, per_device(): lax.all_to_all(outbox, ('term', 'sector'), split_axis=0, concat_axis=0, t...  22.2 us
    pallas_call x1, Pallas kernels, products(): pl.pallas_call(functools.partial(product_kernel, sectors, terms, step), i...  7.19 us
    pallas_call x1, Pallas kernels, combine(): pl.pallas_call(combine_kernel, grid=(peers // step,), in_specs=[pl.BlockS...  2.72 us
  transfers between devices with their start and end apart: 1, of which 1 were waited for; matrix products, arithmetic and copies ran while one was open for 0% of the time, Pallas kernels for 0%

profile of v3, /device:TPU:1, one launch (start us, length us, event | category | flops | bytes accessed | tf_op | source)
XLA Modules:
  0.0 92.6 jit_solution(11476476595864049468)
XLA Ops:
  0.0 7.2 %shard_map.55 = f32[4608,128]{1,0:T(8,128)} custom-call(s32[64]{0:T(128)} %bitcast.8, f32[64,32,128]{2,1,0:T(8,128)} %psi_hbm.1, f32[3,32,32,64]{3,2,1,0:T(8,128)} %bitcast.6, f32[3,128,128]{2,1,0:T(8,128)} %right_hbm.1), custom_call_target="tpu_custom_call" | custom-call | tf_op jit(solution)/shard_map/pallas_call | solution.py:117
  7.2 0.0 copy-start
  7.2 22.2 %all-to-all-start = ((f32[512,9,1,128]{3,2,1,0:T(1,128)}), f32[512,9,1,128]{3,2,1,0:T(1,128)S(1)}, u32[]{:S(2)}, u32[]{:S(2)}) async-start(f32[512,9,1,128]{3,2,1,0:T(1,128)} %bitcast.5), calls=%async_computation | async-start | bytes 4718592 | tf_op jit(solution)/shard_map/all_to_all | solution.py:187
  29.4 0.0 copy-done
  29.4 0.1 copy.6.live_ref
  29.5 60.4 %all-to-all-done.inbox_ref = f32[512,9,1,128]{3,2,1,0:T(1,128)S(1)} async-done(((f32[512,9,1,128]{3,2,1,0:T(1,128)}), f32[512,9,1,128]{3,2,1,0:T(1,128)S(1)}, u32[]{:S(2)}, u32[]{:S(2)}) %all-to-all-start) | async-done | bytes 2359328 | tf_op jit(solution)/shard_map/all_to_all | solution.py:187
  89.9 2.7 %shard_map.56 = f32[64,4,128]{2,1,0:T(4,128)} custom-call(s32[1]{0:T(128)} %bitcast.term_ref, f32[512,9,1,128]{3,2,1,0:T(1,128)S(1)} %all-to-all-done.inbox_ref, s32[64,1]{1,0:T(8,128)S(1)} %copy.6.live_ref), custom_call_target="tpu_custom_call" | custom-call | tf_op jit(solution)/shard_map/pallas_call | solution.py:168
Async XLA Ops:
  7.2 22.2 %copy-start = (s32[64]{0:T(128)S(1)}, s32[64]{0:T(128)}, u32[]{:S(2)}) copy-start(s32[64]{0:T(128)} %param.9) | copy-start | bytes 772
  7.2 82.7 %all-to-all-start = ((f32[512,9,1,128]{3,2,1,0:T(1,128)}), f32[512,9,1,128]{3,2,1,0:T(1,128)S(1)}, u32[]{:S(2)}, u32[]{:S(2)}) async-start(f32[512,9,1,128]{3,2,1,0:T(1,128)} %bitcast.5), calls=%async_computation | async-start | bytes 4718592 | tf_op jit(solution)/shard_map/all_to_all | solution.py:187

commit v4 on v3

--- a/solution.py
+++ b/solution.py
@@ -136,48 +136,42 @@
     return out.reshape(sectors * terms, message, 1, cols)
 
 
-def combine_kernel(term_ref, inbox_ref, live_ref, out_ref, total):
-    index = pl.program_id(0)
+def combine_kernel(message, term_ref, inbox_ref, live_ref, out_ref, total):
     cols = inbox_ref.shape[-1]
     blocks, rows = out_ref.shape[0], out_ref.shape[1]
+    peers = inbox_ref.shape[0] // message
+    step = 128
+    for index in range(peers // step):
 
-    @pl.when(index == 0)
-    def begin():
-        total[...] = jnp.zeros_like(total)
+        def row(r):
+            return inbox_ref[pl.ds(index * step * message + r, step, stride=message), :]
 
-    marks = inbox_ref[:, 2 * rows, 0, :].astype(BF16)
-    for slot in range(2):
-        got = jnp.concatenate([inbox_ref[:, slot * rows + r, 0, :] for r in range(rows)], axis=1)
-        high, low = halves(got)
-        select = marks[:, slot * blocks : (slot + 1) * blocks]
-        dims = (((0,), (0,)), ((), ()))
-        total[...] += lax.dot_general(select, high, dims, preferred_element_type=F32)
-        total[...] += lax.dot_general(select, low, dims, preferred_element_type=F32)
-
-    @pl.when(index == pl.num_programs(0) - 1)
-    def end():
+        select = row(2 * rows).astype(BF16).T
+        select = jnp.concatenate([select[:blocks], select[blocks:]], axis=1)
         for r in range(rows):
-            alive = term_ref[0] * rows + r < live_ref[...]
-            out_ref[:, r, :] = jnp.where(alive, total[:, r * cols : (r + 1) * cols], 0.0)
+            got = jnp.concatenate([row(r), row(rows + r)], axis=0)
+            high, low = halves(got)
+            both = jnp.dot(select, jnp.concatenate([high, low], axis=1), preferred_element_type=F32)
+            value = both[:, :cols] + both[:, cols:]
+            at = slice(r * cols, (r + 1) * cols)
+            total[:, at] = value if index == 0 else total[:, at] + value
+    for r in range(rows):
+        alive = term_ref[0] * rows + r < live_ref[...]
+        out_ref[:, r, :] = jnp.where(alive, total[:, r * cols : (r + 1) * cols], 0.0)
 
 
 def combine(term, inbox, block_rows, rows):
     peers, message, _, cols = inbox.shape
     blocks = block_rows.shape[0]
-    step = 128
+    vmem = pl.BlockSpec(memory_space=pltpu.VMEM)
     return pl.pallas_call(
-        combine_kernel,
-        grid=(peers // step,),
-        in_specs=[
-            pl.BlockSpec(memory_space=pltpu.SMEM),
-            pl.BlockSpec((step, message, 1, cols), lambda i: (i, 0, 0, 0)),
-            pl.BlockSpec((blocks, 1), lambda i: (0, 0)),
-        ],
-        out_specs=pl.BlockSpec((blocks, rows, cols), lambda i: (0, 0, 0)),
+        functools.partial(combine_kernel, message),
+        in_specs=[pl.BlockSpec(memory_space=pltpu.SMEM), vmem, vmem],
+        out_specs=vmem,
         out_shape=jax.ShapeDtypeStruct((blocks, rows, cols), F32),
         scratch_shapes=[pltpu.VMEM((blocks, rows * cols), F32)],
         compiler_params=pltpu.CompilerParams(vmem_limit_bytes=40 * 1024 * 1024),
-    )(term, inbox, block_rows.reshape(blocks, 1))
+    )(term, inbox.reshape(peers * message, cols), block_rows.reshape(blocks, 1))
 
 
 def per_device(psi, left_env, right_env, dest, block_rows):

time: 92.8 us -> 91.3 us (0.984)
  Pallas kernels: 9.91 us -> 8.39 us
    pallas_call x1, Pallas kernels: 2.72 us -> 1.21 us  [combine(): pl.pallas_call(functools.partial(combine_kernel, message), in_specs=[pl.B...]
where the time goes in v4:
time: 91.3 us; the launch traced here: 91.1 us
  waiting for transfers between devices  60.4 us (66%)
  starting transfers between devices  22.2 us (24%)
  Pallas kernels  8.39 us (9%)
    all_to_all x1, waiting for transfers between devices, per_device(): lax.all_to_all(outbox, ('term', 'sector'), split_axis=0, concat_axis=0, t...  60.4 us
    all_to_all x1, starting transfers between devices, per_device(): lax.all_to_all(outbox, ('term', 'sector'), split_axis=0, concat_axis=0, t...  22.2 us
    pallas_call x1, Pallas kernels, products(): pl.pallas_call(functools.partial(product_kernel, sectors, terms, step), i...  7.19 us
  transfers between devices with their start and end apart: 1, of which 1 were waited for; matrix products, arithmetic and copies ran while one was open for 0% of the time, Pallas kernels for 0%

profile of v4, /device:TPU:1, one launch (start us, length us, event | category | flops | bytes accessed | tf_op | source)
XLA Modules:
  0.0 91.1 jit_solution(10522997356926887469)
XLA Ops:
  0.0 7.2 %shard_map.55 = f32[4608,128]{1,0:T(8,128)} custom-call(s32[64]{0:T(128)} %bitcast.10, f32[64,32,128]{2,1,0:T(8,128)} %psi_hbm.1, f32[3,32,32,64]{3,2,1,0:T(8,128)} %bitcast.8, f32[3,128,128]{2,1,0:T(8,128)} %right_hbm.1), custom_call_target="tpu_custom_call" | custom-call | tf_op jit(solution)/shard_map/pallas_call | solution.py:117
  7.2 0.0 copy-start
  7.2 22.2 %all-to-all-start = ((f32[512,9,1,128]{3,2,1,0:T(1,128)}), f32[512,9,1,128]{3,2,1,0:T(1,128)S(1)}, u32[]{:S(2)}, u32[]{:S(2)}) async-start(f32[512,9,1,128]{3,2,1,0:T(1,128)} %bitcast.7), calls=%async_computation | async-start | bytes 4718592 | tf_op jit(solution)/shard_map/all_to_all | solution.py:181
  29.4 0.0 copy-done
  29.4 0.1 copy.9.live_ref
  29.5 60.4 %all-to-all-done = f32[512,9,1,128]{3,2,1,0:T(1,128)S(1)} async-done(((f32[512,9,1,128]{3,2,1,0:T(1,128)}), f32[512,9,1,128]{3,2,1,0:T(1,128)S(1)}, u32[]{:S(2)}, u32[]{:S(2)}) %all-to-all-start) | async-done | bytes 2359328 | tf_op jit(solution)/shard_map/all_to_all | solution.py:181
  89.9 1.2 %shard_map.56 = f32[64,4,128]{2,1,0:T(4,128)} custom-call(s32[1]{0:T(128)} %bitcast.term_ref, f32[4608,128]{1,0:T(8,128)S(1)} %bitcast.6, s32[64,1]{1,0:T(8,128)S(1)} %copy.9.live_ref), custom_call_target="tpu_custom_call" | custom-call | tf_op jit(solution)/shard_map/pallas_call | solution.py:167
Async XLA Ops:
  7.2 22.2 %copy-start = (s32[64]{0:T(128)S(1)}, s32[64]{0:T(128)}, u32[]{:S(2)}) copy-start(s32[64]{0:T(128)} %param.9) | copy-start | bytes 772
  7.2 82.7 %all-to-all-start = ((f32[512,9,1,128]{3,2,1,0:T(1,128)}), f32[512,9,1,128]{3,2,1,0:T(1,128)S(1)}, u32[]{:S(2)}, u32[]{:S(2)}) async-start(f32[512,9,1,128]{3,2,1,0:T(1,128)} %bitcast.7), calls=%async_computation | async-start | bytes 4718592 | tf_op jit(solution)/shard_map/all_to_all | solution.py:181

commit v5 on v4

--- a/solution.py
+++ b/solution.py
@@ -16,23 +16,30 @@
 
 
 def product_kernel(
-    sectors, terms, step,
+    sectors, terms,
     dest_ref, psi_hbm, left_hbm, right_hbm, out_hbm,
-    psi, left, right, turned, rights, counts, inner, outbox, marks, sems,
+    psi, left, right, turned, rights, counts, outbox, marks, middle, sems,
 ):
     blocks, rows, cols = psi.shape
     share = right.shape[0]
     held = rows // terms
     message = 2 * held + 1
-    pack = cols // rows
-    groups = share * rows // pack
-
-    fetches = [
-        pltpu.make_async_copy(left_hbm, left, sems.at[0]),
-        pltpu.make_async_copy(right_hbm, right, sems.at[1]),
-        pltpu.make_async_copy(psi_hbm, psi, sems.at[2]),
-    ]
-    for fetch in fetches:
+
+    fetch_right = pltpu.make_async_copy(right_hbm, right, sems.at[0])
+    step, span = blocks // 2, rows // 1
+    fetch_psi, fetch_left = [], []
+    for i in range(2):
+        part = pl.ds(i * step, step)
+        fetch_psi.append(pltpu.make_async_copy(psi_hbm.at[part], psi.at[part], sems.at[1 + i]))
+    for i in range(1):
+        part = pl.ds(i * span, span)
+        fetch_left.append(
+            pltpu.make_async_copy(left_hbm.at[:, part], left.at[:, part], sems.at[1 + 2 + i])
+        )
+    fetch_right.start()
+    for fetch in fetch_psi:
+        fetch.start()
+    for fetch in fetch_left:
         fetch.start()
 
     outbox[...] = jnp.zeros_like(outbox)
@@ -44,61 +51,61 @@
 
     lax.fori_loop(0, sectors, clear, 0)
 
-    fetches[0].wait()
-    for g in range(groups):
-        slabs = []
-        for j in range(pack):
-            at = j * groups + g
-            slabs.append(left[at // rows, at % rows])
-        slab = jnp.concatenate(slabs, axis=0)
-        turned[g * blocks : (g + 1) * blocks, :] = slab.T
-    fetches[1].wait()
+    fetch_right.wait()
     for k in range(share):
         high, low = halves(right[k])
-        rights[k * cols : (k + 1) * cols, :cols] = high
-        rights[k * cols : (k + 1) * cols, cols:] = low
-    fetches[2].wait()
+        rights[:cols, k * cols : (k + 1) * cols] = high
+        rights[cols : 2 * cols, k * cols : (k + 1) * cols] = high
+        rights[2 * cols :, k * cols : (k + 1) * cols] = low
+
+    def first(index, carry):
+        value = psi[pl.ds(index * step, step)].reshape(step * rows, cols)
+        high, low = halves(value)
+        stacked = jnp.concatenate([high, low, high], axis=1)
+        value = jnp.dot(stacked, rights[...], preferred_element_type=F32)
+        high, low = halves(value)
+        for b in range(step):
+            for k in range(share):
+                at = slice(k * rows, (k + 1) * rows)
+                part = (slice(b * rows, (b + 1) * rows), slice(k * cols, (k + 1) * cols))
+                middle[index * step + b, at, :cols] = high[part]
+                middle[index * step + b, at, cols:] = low[part]
+        return carry
+
+    for index, fetch in enumerate(fetch_psi):
+        fetch.wait()
+        first(index, 0)
+
+    for r in range(rows):
+        if r % span == 0:
+            fetch_left[r // span].wait()
+        slab = jnp.concatenate([left[k, r] for k in range(share)], axis=0)
+        turned[r * blocks : (r + 1) * blocks, :] = slab.T
 
     lane = lax.broadcasted_iota(jnp.int32, (1, cols), 1)
-    wide = lax.broadcasted_iota(jnp.int32, (groups, cols), 1)
-    front, even = wide < cols // 2, (wide // rows) % 2 == 0
-
-    def chunk(index, carry):
+
+    def second(index, carry):
         for b in range(step):
             q = index * step + b
-            mine = turned[pl.ds(q, groups, stride=blocks), :]
-            high = mine.astype(BF16).astype(F32)
-            low = mine - high
-            highs = [high] + [pltpu.roll(high, rows * m, 1) for m in range(1, pack)]
-            lows = [low] + [pltpu.roll(low, rows * m, 1) for m in range(1, pack)]
-            parts = []
-            for j in range(pack):
-                h = jnp.where(front, highs[-j % pack], highs[(2 - j) % pack])
-                l = jnp.where(front, lows[(1 - j) % pack], lows[(3 - j) % pack])
-                parts.append(jnp.where(even, h, l))
-            lefts = jnp.concatenate(parts, axis=0).astype(BF16)
-            psi_high, psi_low = halves(psi[q])
-            psis = jnp.concatenate([psi_high, psi_high, psi_low, psi_low], axis=0)
-            value = jnp.dot(lefts, psis, preferred_element_type=F32)
-            for k in range(share):
-                inner[b * rows : (b + 1) * rows, k * cols : (k + 1) * cols] = value[k * rows : (k + 1) * rows]
-        high, low = halves(inner[...])
-        both = jnp.dot(high, rights[...], preferred_element_type=F32)
-        items = both[:, :cols] + both[:, cols:]
-        items = items + jnp.dot(low, rights[:, :cols], preferred_element_type=F32)
-        for b in range(step):
-            target = dest_ref[index * step + b]
+            high, low = halves(turned[pl.ds(q, rows, stride=blocks), :])
+            both = jnp.dot(
+                jnp.concatenate([high, low], axis=0), middle[q], preferred_element_type=F32
+            )
+            item = both[:rows, :cols] + (both[:rows, cols:] + both[rows:, :cols])
+            target = dest_ref[q]
             owner, local = target // blocks, target % blocks
             slot = counts[owner]
             counts[owner] = slot + 1
             marks[pl.ds(owner, 1), :] += (lane == slot * blocks + local).astype(F32)
             base = owner * message + slot * held
             for piece in range(terms):
-                row = b * rows + piece * held
-                outbox[pl.ds(base + piece * sectors * message, held), :] = items[row : row + held]
+                outbox[pl.ds(base + piece * sectors * message, held), :] = item[
+                    piece * held : (piece + 1) * held
+                ]
         return carry
 
-    lax.fori_loop(0, blocks // step, chunk, 0)
+    for index in range(blocks // step):
+        second(index, 0)
     for piece in range(terms):
         at = piece * sectors * message + 2 * held
         outbox[pl.ds(at, sectors, stride=message), :] = marks[...]
@@ -110,12 +117,11 @@
 def products(dest, psi, left_env, right_env, sectors, terms):
     blocks, rows, cols = psi.shape
     share = right_env.shape[0]
-    step = 16
     message = 2 * (rows // terms) + 1
     total = sectors * terms * message
     hbm = pl.BlockSpec(memory_space=pltpu.HBM)
     out = pl.pallas_call(
-        functools.partial(product_kernel, sectors, terms, step),
+        functools.partial(product_kernel, sectors, terms),
         in_specs=[pl.BlockSpec(memory_space=pltpu.SMEM), hbm, hbm, hbm],
         out_specs=hbm,
         out_shape=jax.ShapeDtypeStruct((total, cols), F32),
@@ -123,13 +129,13 @@
             pltpu.VMEM((blocks, rows, cols), F32),
             pltpu.VMEM((share, rows, rows, blocks), F32),
             pltpu.VMEM((share, cols, cols), F32),
-            pltpu.VMEM((share * rows * rows * blocks // cols, cols), F32),
-            pltpu.VMEM((share * cols, 2 * cols), BF16),
+            pltpu.VMEM((rows * blocks, share * rows), F32),
+            pltpu.VMEM((3 * cols, share * cols), BF16),
             pltpu.SMEM((sectors,), jnp.int32),
-            pltpu.VMEM((step * rows, share * cols), F32),
             pltpu.VMEM((total, cols), F32),
             pltpu.VMEM((sectors, cols), F32),
-            pltpu.SemaphoreType.DMA((3,)),
+            pltpu.VMEM((blocks, share * rows, 2 * cols), BF16),
+            pltpu.SemaphoreType.DMA((4,)),
         ],
         compiler_params=pltpu.CompilerParams(vmem_limit_bytes=60 * 1024 * 1024),
     )(dest, psi, jnp.transpose(left_env, (1, 2, 3, 0)), right_env)

time: 91.3 us -> 90.5 us (level)
  no operation moved by 1% of the time
where the time goes in v5:
time: 90.5 us; the launch traced here: 90.4 us
  waiting for transfers between devices  60.4 us (67%)
  starting transfers between devices  22.2 us (25%)
  Pallas kernels  7.64 us (8%)
    all_to_all x1, waiting for transfers between devices, per_device(): lax.all_to_all(outbox, ('term', 'sector'), split_axis=0, concat_axis=0, t...  60.4 us
    all_to_all x1, starting transfers between devices, per_device(): lax.all_to_all(outbox, ('term', 'sector'), split_axis=0, concat_axis=0, t...  22.2 us
    pallas_call x1, Pallas kernels, products(): pl.pallas_call(functools.partial(product_kernel, sectors, terms), in_spec...  6.43 us
  transfers between devices with their start and end apart: 1, of which 1 were waited for; matrix products, arithmetic and copies ran while one was open for 0% of the time, Pallas kernels for 0%

profile of v5, /device:TPU:1, one launch (start us, length us, event | category | flops | bytes accessed | tf_op | source)
XLA Modules:
  0.0 90.4 jit_solution(7108766345259445137)
XLA Ops:
  0.0 6.4 %shard_map.55 = f32[4608,128]{1,0:T(8,128)} custom-call(s32[64]{0:T(128)} %bitcast.10, f32[64,32,128]{2,1,0:T(8,128)} %psi_hbm.1, f32[3,32,32,64]{3,2,1,0:T(8,128)} %bitcast.8, f32[3,128,128]{2,1,0:T(8,128)} %right_hbm.1), custom_call_target="tpu_custom_call" | custom-call | tf_op jit(solution)/shard_map/pallas_call | solution.py:123
  6.4 0.0 copy-start
  6.5 22.2 %all-to-all-start = ((f32[512,9,1,128]{3,2,1,0:T(1,128)}), f32[512,9,1,128]{3,2,1,0:T(1,128)S(1)}, u32[]{:S(2)}, u32[]{:S(2)}) async-start(f32[512,9,1,128]{3,2,1,0:T(1,128)} %bitcast.7), calls=%async_computation | async-start | bytes 4718592 | tf_op jit(solution)/shard_map/all_to_all | solution.py:187
  28.6 0.0 copy-done
  28.6 0.1 copy.9.live_ref
  28.7 60.4 %all-to-all-done = f32[512,9,1,128]{3,2,1,0:T(1,128)S(1)} async-done(((f32[512,9,1,128]{3,2,1,0:T(1,128)}), f32[512,9,1,128]{3,2,1,0:T(1,128)S(1)}, u32[]{:S(2)}, u32[]{:S(2)}) %all-to-all-start) | async-done | bytes 2359328 | tf_op jit(solution)/shard_map/all_to_all | solution.py:187
  89.2 1.2 %shard_map.56 = f32[64,4,128]{2,1,0:T(4,128)} custom-call(s32[1]{0:T(128)} %bitcast.term_ref, f32[4608,128]{1,0:T(8,128)S(1)} %bitcast.6, s32[64,1]{1,0:T(8,128)S(1)} %copy.9.live_ref), custom_call_target="tpu_custom_call" | custom-call | tf_op jit(solution)/shard_map/pallas_call | solution.py:173
Async XLA Ops:
  6.4 22.2 %copy-start = (s32[64]{0:T(128)S(1)}, s32[64]{0:T(128)}, u32[]{:S(2)}) copy-start(s32[64]{0:T(128)} %param.9) | copy-start | bytes 772
  6.5 82.7 %all-to-all-start = ((f32[512,9,1,128]{3,2,1,0:T(1,128)}), f32[512,9,1,128]{3,2,1,0:T(1,128)S(1)}, u32[]{:S(2)}, u32[]{:S(2)}) async-start(f32[512,9,1,128]{3,2,1,0:T(1,128)} %bitcast.7), calls=%async_computation | async-start | bytes 4718592 | tf_op jit(solution)/shard_map/all_to_all | solution.py:187

commit v6 on v5

--- a/solution.py
+++ b/solution.py
@@ -18,7 +18,7 @@
 def product_kernel(
     sectors, terms,
     dest_ref, psi_hbm, left_hbm, right_hbm, out_hbm,
-    psi, left, right, turned, rights, counts, outbox, marks, middle, sems,
+    psi, left, right, turned, rights, counts, places, outbox, marks, middle, sems,
 ):
     blocks, rows, cols = psi.shape
     share = right.shape[0]
@@ -26,21 +26,16 @@
     message = 2 * held + 1
 
     fetch_right = pltpu.make_async_copy(right_hbm, right, sems.at[0])
-    step, span = blocks // 2, rows // 1
-    fetch_psi, fetch_left = [], []
+    fetch_left = pltpu.make_async_copy(left_hbm, left, sems.at[1])
+    fetch_psi = []
+    step = blocks // 2
     for i in range(2):
         part = pl.ds(i * step, step)
-        fetch_psi.append(pltpu.make_async_copy(psi_hbm.at[part], psi.at[part], sems.at[1 + i]))
-    for i in range(1):
-        part = pl.ds(i * span, span)
-        fetch_left.append(
-            pltpu.make_async_copy(left_hbm.at[:, part], left.at[:, part], sems.at[1 + 2 + i])
-        )
+        fetch_psi.append(pltpu.make_async_copy(psi_hbm.at[part], psi.at[part], sems.at[2 + i]))
     fetch_right.start()
     for fetch in fetch_psi:
         fetch.start()
-    for fetch in fetch_left:
-        fetch.start()
+    fetch_left.start()
 
     outbox[...] = jnp.zeros_like(outbox)
     marks[...] = jnp.zeros_like(marks)
@@ -76,42 +71,43 @@
         fetch.wait()
         first(index, 0)
 
+    fetch_left.wait()
     for r in range(rows):
-        if r % span == 0:
-            fetch_left[r // span].wait()
         slab = jnp.concatenate([left[k, r] for k in range(share)], axis=0)
         turned[r * blocks : (r + 1) * blocks, :] = slab.T
 
     lane = lax.broadcasted_iota(jnp.int32, (1, cols), 1)
-
-    def second(index, carry):
-        for b in range(step):
-            q = index * step + b
-            high, low = halves(turned[pl.ds(q, rows, stride=blocks), :])
+    for q in range(blocks):
+        target = dest_ref[q]
+        owner, local = target // blocks, target % blocks
+        slot = counts[owner]
+        counts[owner] = slot + 1
+        places[q] = owner * message + slot * held
+        marks[pl.ds(owner, 1), :] += (lane == slot * blocks + local).astype(F32)
+
+    span = rows // 2
+    pushes = []
+    for begin in range(0, rows, span):
+        for q in range(blocks):
+            mine = turned[pl.ds(begin * blocks + q, span, stride=blocks), :]
+            high, low = halves(mine)
             both = jnp.dot(
                 jnp.concatenate([high, low], axis=0), middle[q], preferred_element_type=F32
             )
-            item = both[:rows, :cols] + (both[:rows, cols:] + both[rows:, :cols])
-            target = dest_ref[q]
-            owner, local = target // blocks, target % blocks
-            slot = counts[owner]
-            counts[owner] = slot + 1
-            marks[pl.ds(owner, 1), :] += (lane == slot * blocks + local).astype(F32)
-            base = owner * message + slot * held
-            for piece in range(terms):
-                outbox[pl.ds(base + piece * sectors * message, held), :] = item[
-                    piece * held : (piece + 1) * held
-                ]
-        return carry
-
-    for index in range(blocks // step):
-        second(index, 0)
-    for piece in range(terms):
-        at = piece * sectors * message + 2 * held
-        outbox[pl.ds(at, sectors, stride=message), :] = marks[...]
-    push = pltpu.make_async_copy(outbox, out_hbm, sems.at[0])
-    push.start()
-    push.wait()
+            item = both[:span, :cols] + (both[:span, cols:] + both[span:, :cols])
+            for at in range(0, span, held):
+                piece = (begin + at) // held
+                outbox[pl.ds(places[q] + piece * sectors * message, held), :] = item[at : at + held]
+        for piece in range(begin // held, (begin + span) // held):
+            at = piece * sectors * message + 2 * held
+            outbox[pl.ds(at, sectors, stride=message), :] = marks[:sectors, :]
+        size = span // held * sectors * message
+        part = pl.ds(begin // held * sectors * message, size)
+        push = pltpu.make_async_copy(outbox.at[part], out_hbm.at[part], sems.at[len(pushes)])
+        push.start()
+        pushes.append(push)
+    for push in pushes:
+        push.wait()
 
 
 def products(dest, psi, left_env, right_env, sectors, terms):
@@ -129,11 +125,12 @@
             pltpu.VMEM((blocks, rows, cols), F32),
             pltpu.VMEM((share, rows, rows, blocks), F32),
             pltpu.VMEM((share, cols, cols), F32),
-            pltpu.VMEM((rows * blocks, share * rows), F32),
+            pltpu.VMEM((rows * blocks + blocks, share * rows), F32),
             pltpu.VMEM((3 * cols, share * cols), BF16),
             pltpu.SMEM((sectors,), jnp.int32),
-            pltpu.VMEM((total, cols), F32),
-            pltpu.VMEM((sectors, cols), F32),
+            pltpu.SMEM((blocks,), jnp.int32),
+            pltpu.VMEM((total + 8, cols), F32),
+            pltpu.VMEM((sectors + 8, cols), F32),
             pltpu.VMEM((blocks, share * rows, 2 * cols), BF16),
             pltpu.SemaphoreType.DMA((4,)),
         ],

time: 90.5 us -> 90.2 us (level)
  no operation moved by 1% of the time
where the time goes in v6:
time: 90.2 us; the launch traced here: 90 us
  waiting for transfers between devices  60.4 us (67%)
  starting transfers between devices  22.2 us (25%)
  Pallas kernels  7.32 us (8%)
    all_to_all x1, waiting for transfers between devices, per_device(): lax.all_to_all(outbox, ('term', 'sector'), split_axis=0, concat_axis=0, t...  60.4 us
    all_to_all x1, starting transfers between devices, per_device(): lax.all_to_all(outbox, ('term', 'sector'), split_axis=0, concat_axis=0, t...  22.2 us
    pallas_call x1, Pallas kernels, products(): pl.pallas_call(functools.partial(product_kernel, sectors, terms), in_spec...  6.11 us
  transfers between devices with their start and end apart: 1, of which 1 were waited for; matrix products, arithmetic and copies ran while one was open for 0% of the time, Pallas kernels for 0%

profile of v6, /device:TPU:1, one launch (start us, length us, event | category | flops | bytes accessed | tf_op | source)
XLA Modules:
  0.0 90.0 jit_solution(8668799113357236815)
XLA Ops:
  0.0 6.1 %shard_map.55 = f32[4608,128]{1,0:T(8,128)} custom-call(s32[64]{0:T(128)} %bitcast.10, f32[64,32,128]{2,1,0:T(8,128)} %psi_hbm.1, f32[3,32,32,64]{3,2,1,0:T(8,128)} %bitcast.8, f32[3,128,128]{2,1,0:T(8,128)} %right_hbm.1), custom_call_target="tpu_custom_call" | custom-call | tf_op jit(solution)/shard_map/pallas_call | solution.py:119
  6.1 0.0 copy-start
  6.1 22.2 %all-to-all-start = ((f32[512,9,1,128]{3,2,1,0:T(1,128)}), f32[512,9,1,128]{3,2,1,0:T(1,128)S(1)}, u32[]{:S(2)}, u32[]{:S(2)}) async-start(f32[512,9,1,128]{3,2,1,0:T(1,128)} %bitcast.7), calls=%async_computation | async-start | bytes 4718592 | tf_op jit(solution)/shard_map/all_to_all | solution.py:184
  28.3 0.0 copy-done
  28.3 0.1 copy.9.live_ref
  28.4 60.4 %all-to-all-done = f32[512,9,1,128]{3,2,1,0:T(1,128)S(1)} async-done(((f32[512,9,1,128]{3,2,1,0:T(1,128)}), f32[512,9,1,128]{3,2,1,0:T(1,128)S(1)}, u32[]{:S(2)}, u32[]{:S(2)}) %all-to-all-start) | async-done | bytes 2359328 | tf_op jit(solution)/shard_map/all_to_all | solution.py:184
  88.8 1.2 %shard_map.56 = f32[64,4,128]{2,1,0:T(4,128)} custom-call(s32[1]{0:T(128)} %bitcast.term_ref, f32[4608,128]{1,0:T(8,128)S(1)} %bitcast.6, s32[64,1]{1,0:T(8,128)S(1)} %copy.9.live_ref), custom_call_target="tpu_custom_call" | custom-call | tf_op jit(solution)/shard_map/pallas_call | solution.py:170
Async XLA Ops:
  6.1 22.2 %copy-start = (s32[64]{0:T(128)S(1)}, s32[64]{0:T(128)}, u32[]{:S(2)}) copy-start(s32[64]{0:T(128)} %param.9) | copy-start | bytes 772
  6.1 82.7 %all-to-all-start = ((f32[512,9,1,128]{3,2,1,0:T(1,128)}), f32[512,9,1,128]{3,2,1,0:T(1,128)S(1)}, u32[]{:S(2)}, u32[]{:S(2)}) async-start(f32[512,9,1,128]{3,2,1,0:T(1,128)} %bitcast.7), calls=%async_computation | async-start | bytes 4718592 | tf_op jit(solution)/shard_map/all_to_all | solution.py:184

commit v7 on v6

--- a/solution.py
+++ b/solution.py
@@ -82,32 +82,25 @@
         owner, local = target // blocks, target % blocks
         slot = counts[owner]
         counts[owner] = slot + 1
-        places[q] = owner * message + slot * held
+        places[q] = owner * terms * message + slot * held
         marks[pl.ds(owner, 1), :] += (lane == slot * blocks + local).astype(F32)
 
-    span = rows // 2
-    pushes = []
-    for begin in range(0, rows, span):
-        for q in range(blocks):
-            mine = turned[pl.ds(begin * blocks + q, span, stride=blocks), :]
-            high, low = halves(mine)
-            both = jnp.dot(
-                jnp.concatenate([high, low], axis=0), middle[q], preferred_element_type=F32
-            )
-            item = both[:span, :cols] + (both[:span, cols:] + both[span:, :cols])
-            for at in range(0, span, held):
-                piece = (begin + at) // held
-                outbox[pl.ds(places[q] + piece * sectors * message, held), :] = item[at : at + held]
-        for piece in range(begin // held, (begin + span) // held):
-            at = piece * sectors * message + 2 * held
-            outbox[pl.ds(at, sectors, stride=message), :] = marks[:sectors, :]
-        size = span // held * sectors * message
-        part = pl.ds(begin // held * sectors * message, size)
-        push = pltpu.make_async_copy(outbox.at[part], out_hbm.at[part], sems.at[len(pushes)])
-        push.start()
-        pushes.append(push)
-    for push in pushes:
-        push.wait()
+    for q in range(blocks):
+        high, low = halves(turned[pl.ds(q, rows, stride=blocks), :])
+        both = jnp.dot(
+            jnp.concatenate([high, low], axis=0), middle[q], preferred_element_type=F32
+        )
+        item = both[:rows, :cols] + (both[:rows, cols:] + both[rows:, :cols])
+        for piece in range(terms):
+            at = places[q] + piece * message
+            outbox[pl.ds(at, held), :] = item[piece * held : (piece + 1) * held]
+    for piece in range(terms):
+        at = piece * message + 2 * held
+        outbox[pl.ds(at, sectors, stride=terms * message), :] = marks[:sectors, :]
+    total = sectors * terms * message
+    push = pltpu.make_async_copy(outbox.at[pl.ds(0, total)], out_hbm, sems.at[0])
+    push.start()
+    push.wait()
 
 
 def products(dest, psi, left_env, right_env, sectors, terms):
@@ -181,7 +174,7 @@
     sectors, terms = lax.axis_size("sector"), lax.axis_size("term")
     rows = psi.shape[1] // terms
     outbox = products(dest.reshape(-1), psi, left_env, right_env, sectors, terms)
-    inbox = lax.all_to_all(outbox, ("term", "sector"), split_axis=0, concat_axis=0, tiled=True)
+    inbox = lax.all_to_all(outbox, ("sector", "term"), split_axis=0, concat_axis=0, tiled=True)
     term = lax.axis_index("term").reshape(1)
     return combine(term, inbox, block_rows, rows)
 

time: 90.2 us -> 89.1 us (0.988)
  waiting for transfers between devices: 60.4 us -> 59 us
    all_to_all x1, waiting for transfers between devices: 60.4 us -> 59 us  [per_device(): lax.all_to_all(outbox, ('sector', 'term'), split_axis=0, concat_axis=0, t...]
where the time goes in v7:
time: 89.1 us; the launch traced here: 88.9 us
  waiting for transfers between devices  59 us (66%)
  starting transfers between devices  22.2 us (25%)
  Pallas kernels  7.63 us (9%)
    all_to_all x1, waiting for transfers between devices, per_device(): lax.all_to_all(outbox, ('sector', 'term'), split_axis=0, concat_axis=0, t...  59 us
    all_to_all x1, starting transfers between devices, per_device(): lax.all_to_all(outbox, ('sector', 'term'), split_axis=0, concat_axis=0, t...  22.2 us
    pallas_call x1, Pallas kernels, products(): pl.pallas_call(functools.partial(product_kernel, sectors, terms), in_spec...  6.42 us
  transfers between devices with their start and end apart: 1, of which 1 were waited for; matrix products, arithmetic and copies ran while one was open for 0% of the time, Pallas kernels for 0%

profile of v7, /device:TPU:1, one launch (start us, length us, event | category | flops | bytes accessed | tf_op | source)
XLA Modules:
  0.0 88.9 jit_solution(15466158247538467313)
XLA Ops:
  0.0 6.4 %shard_map.55 = f32[4608,128]{1,0:T(8,128)} custom-call(s32[64]{0:T(128)} %bitcast.10, f32[64,32,128]{2,1,0:T(8,128)} %psi_hbm.1, f32[3,32,32,64]{3,2,1,0:T(8,128)} %bitcast.8, f32[3,128,128]{2,1,0:T(8,128)} %right_hbm.1), custom_call_target="tpu_custom_call" | custom-call | tf_op jit(solution)/shard_map/pallas_call | solution.py:112
  6.4 0.0 copy-start
  6.4 22.2 %all-to-all-start = ((f32[512,9,1,128]{3,2,1,0:T(1,128)}), f32[512,9,1,128]{3,2,1,0:T(1,128)S(1)}, u32[]{:S(2)}, u32[]{:S(2)}) async-start(f32[512,9,1,128]{3,2,1,0:T(1,128)} %bitcast.7), calls=%async_computation | async-start | bytes 4718592 | tf_op jit(solution)/shard_map/all_to_all | solution.py:177
  28.6 0.0 copy-done
  28.6 0.1 copy.9.live_ref
  28.7 59.0 %all-to-all-done = f32[512,9,1,128]{3,2,1,0:T(1,128)S(1)} async-done(((f32[512,9,1,128]{3,2,1,0:T(1,128)}), f32[512,9,1,128]{3,2,1,0:T(1,128)S(1)}, u32[]{:S(2)}, u32[]{:S(2)}) %all-to-all-start) | async-done | bytes 2359328 | tf_op jit(solution)/shard_map/all_to_all | solution.py:177
  87.7 1.2 %shard_map.56 = f32[64,4,128]{2,1,0:T(4,128)} custom-call(s32[1]{0:T(128)} %bitcast.term_ref, f32[4608,128]{1,0:T(8,128)S(1)} %bitcast.6, s32[64,1]{1,0:T(8,128)S(1)} %copy.9.live_ref), custom_call_target="tpu_custom_call" | custom-call | tf_op jit(solution)/shard_map/pallas_call | solution.py:163
Async XLA Ops:
  6.4 22.2 %copy-start = (s32[64]{0:T(128)S(1)}, s32[64]{0:T(128)}, u32[]{:S(2)}) copy-start(s32[64]{0:T(128)} %param.9) | copy-start | bytes 772
  6.4 81.2 %all-to-all-start = ((f32[512,9,1,128]{3,2,1,0:T(1,128)}), f32[512,9,1,128]{3,2,1,0:T(1,128)S(1)}, u32[]{:S(2)}, u32[]{:S(2)}) async-start(f32[512,9,1,128]{3,2,1,0:T(1,128)} %bitcast.7), calls=%async_computation | async-start | bytes 4718592 | tf_op jit(solution)/shard_map/all_to_all | solution.py:177

commit v8 on v7

--- a/solution.py
+++ b/solution.py
@@ -122,7 +122,7 @@
             pltpu.VMEM((3 * cols, share * cols), BF16),
             pltpu.SMEM((sectors,), jnp.int32),
             pltpu.SMEM((blocks,), jnp.int32),
-            pltpu.VMEM((total + 8, cols), F32),
+            pltpu.VMEM((total + terms * message + 8, cols), F32),
             pltpu.VMEM((sectors + 8, cols), F32),
             pltpu.VMEM((blocks, share * rows, 2 * cols), BF16),
             pltpu.SemaphoreType.DMA((4,)),

time: 89.1 us -> 89.1 us (level)
  no operation moved by 1% of the time
where the time goes in v8:
time: 89.1 us; the launch traced here: 88.9 us
  waiting for transfers between devices  59 us (66%)
  starting transfers between devices  22.2 us (25%)
  Pallas kernels  7.63 us (9%)
    all_to_all x1, waiting for transfers between devices, per_device(): lax.all_to_all(outbox, ('sector', 'term'), split_axis=0, concat_axis=0, t...  59 us
    all_to_all x1, starting transfers between devices, per_device(): lax.all_to_all(outbox, ('sector', 'term'), split_axis=0, concat_axis=0, t...  22.2 us
    pallas_call x1, Pallas kernels, products(): pl.pallas_call(functools.partial(product_kernel, sectors, terms), in_spec...  6.42 us
  transfers between devices with their start and end apart: 1, of which 1 were waited for; matrix products, arithmetic and copies ran while one was open for 0% of the time, Pallas kernels for 0%

profile of v8, /device:TPU:1, one launch (start us, length us, event | category | flops | bytes accessed | tf_op | source)
XLA Modules:
  0.0 88.9 jit_solution(7059974928337250314)
XLA Ops:
  0.0 6.4 %shard_map.55 = f32[4608,128]{1,0:T(8,128)} custom-call(s32[64]{0:T(128)} %bitcast.10, f32[64,32,128]{2,1,0:T(8,128)} %psi_hbm.1, f32[3,32,32,64]{3,2,1,0:T(8,128)} %bitcast.8, f32[3,128,128]{2,1,0:T(8,128)} %right_hbm.1), custom_call_target="tpu_custom_call" | custom-call | tf_op jit(solution)/shard_map/pallas_call | solution.py:112
  6.4 0.0 copy-start
  6.4 22.2 %all-to-all-start = ((f32[512,9,1,128]{3,2,1,0:T(1,128)}), f32[512,9,1,128]{3,2,1,0:T(1,128)S(1)}, u32[]{:S(2)}, u32[]{:S(2)}) async-start(f32[512,9,1,128]{3,2,1,0:T(1,128)} %bitcast.7), calls=%async_computation | async-start | bytes 4718592 | tf_op jit(solution)/shard_map/all_to_all | solution.py:177
  28.6 0.0 copy-done
  28.6 0.1 copy.9.live_ref
  28.7 59.0 %all-to-all-done = f32[512,9,1,128]{3,2,1,0:T(1,128)S(1)} async-done(((f32[512,9,1,128]{3,2,1,0:T(1,128)}), f32[512,9,1,128]{3,2,1,0:T(1,128)S(1)}, u32[]{:S(2)}, u32[]{:S(2)}) %all-to-all-start) | async-done | bytes 2359328 | tf_op jit(solution)/shard_map/all_to_all | solution.py:177
  87.7 1.2 %shard_map.56 = f32[64,4,128]{2,1,0:T(4,128)} custom-call(s32[1]{0:T(128)} %bitcast.term_ref, f32[4608,128]{1,0:T(8,128)S(1)} %bitcast.6, s32[64,1]{1,0:T(8,128)S(1)} %copy.9.live_ref), custom_call_target="tpu_custom_call" | custom-call | tf_op jit(solution)/shard_map/pallas_call | solution.py:163
Async XLA Ops:
  6.4 22.2 %copy-start = (s32[64]{0:T(128)S(1)}, s32[64]{0:T(128)}, u32[]{:S(2)}) copy-start(s32[64]{0:T(128)} %param.9) | copy-start | bytes 772
  6.4 81.2 %all-to-all-start = ((f32[512,9,1,128]{3,2,1,0:T(1,128)}), f32[512,9,1,128]{3,2,1,0:T(1,128)S(1)}, u32[]{:S(2)}, u32[]{:S(2)}) async-start(f32[512,9,1,128]{3,2,1,0:T(1,128)} %bitcast.7), calls=%async_computation | async-start | bytes 4718592 | tf_op jit(solution)/shard_map/all_to_all | solution.py:177

commit v9 on v6

--- a/solution.py
+++ b/solution.py
@@ -82,12 +82,13 @@
         owner, local = target // blocks, target % blocks
         slot = counts[owner]
         counts[owner] = slot + 1
-        places[q] = owner * message + slot * held
+        places[q] = owner * terms * message + slot * held
         marks[pl.ds(owner, 1), :] += (lane == slot * blocks + local).astype(F32)
 
-    span = rows // 2
-    pushes = []
-    for begin in range(0, rows, span):
+    outgoing = outbox.reshape(sectors + 1, terms * message, cols)
+    pushes, sent = [], 0
+    for begin, end, ready in ((0, 16, 32), (16, 32, 72)):
+        span = end - begin
         for q in range(blocks):
             mine = turned[pl.ds(begin * blocks + q, span, stride=blocks), :]
             high, low = halves(mine)
@@ -96,16 +97,18 @@
             )
             item = both[:span, :cols] + (both[:span, cols:] + both[span:, :cols])
             for at in range(0, span, held):
-                piece = (begin + at) // held
-                outbox[pl.ds(places[q] + piece * sectors * message, held), :] = item[at : at + held]
-        for piece in range(begin // held, (begin + span) // held):
-            at = piece * sectors * message + 2 * held
-            outbox[pl.ds(at, sectors, stride=message), :] = marks[:sectors, :]
-        size = span // held * sectors * message
-        part = pl.ds(begin // held * sectors * message, size)
-        push = pltpu.make_async_copy(outbox.at[part], out_hbm.at[part], sems.at[len(pushes)])
+                row = places[q] + (begin + at) // held * message
+                outbox[pl.ds(row, held), :] = item[at : at + held]
+        for piece in range(begin // held, end // held):
+            at = piece * message + 2 * held
+            outbox[pl.ds(at, sectors, stride=terms * message), :] = marks[:sectors, :]
+        part = pl.ds(sent, ready - sent)
+        push = pltpu.make_async_copy(
+            outgoing.at[pl.ds(0, sectors), part], out_hbm.at[:, part], sems.at[len(pushes)]
+        )
         push.start()
         pushes.append(push)
+        sent = ready
     for push in pushes:
         push.wait()
 
@@ -120,7 +123,7 @@
         functools.partial(product_kernel, sectors, terms),
         in_specs=[pl.BlockSpec(memory_space=pltpu.SMEM), hbm, hbm, hbm],
         out_specs=hbm,
-        out_shape=jax.ShapeDtypeStruct((total, cols), F32),
+        out_shape=jax.ShapeDtypeStruct((sectors, terms * message, cols), F32),
         scratch_shapes=[
             pltpu.VMEM((blocks, rows, cols), F32),
             pltpu.VMEM((share, rows, rows, blocks), F32),
@@ -129,7 +132,7 @@
             pltpu.VMEM((3 * cols, share * cols), BF16),
             pltpu.SMEM((sectors,), jnp.int32),
             pltpu.SMEM((blocks,), jnp.int32),
-            pltpu.VMEM((total + 8, cols), F32),
+            pltpu.VMEM((total + terms * message, cols), F32),
             pltpu.VMEM((sectors + 8, cols), F32),
             pltpu.VMEM((blocks, share * rows, 2 * cols), BF16),
             pltpu.SemaphoreType.DMA((4,)),
@@ -181,7 +184,7 @@
     sectors, terms = lax.axis_size("sector"), lax.axis_size("term")
     rows = psi.shape[1] // terms
     outbox = products(dest.reshape(-1), psi, left_env, right_env, sectors, terms)
-    inbox = lax.all_to_all(outbox, ("term", "sector"), split_axis=0, concat_axis=0, tiled=True)
+    inbox = lax.all_to_all(outbox, ("sector", "term"), split_axis=0, concat_axis=0, tiled=True)
     term = lax.axis_index("term").reshape(1)
     return combine(term, inbox, block_rows, rows)
 

time: 90.2 us -> 88.9 us (0.986)
  waiting for transfers between devices: 60.4 us -> 59 us
    all_to_all x1, waiting for transfers between devices: 60.4 us -> 59 us  [per_device(): lax.all_to_all(outbox, ('sector', 'term'), split_axis=0, concat_axis=0, t...]
where the time goes in v9:
time: 88.9 us; the launch traced here: 88.7 us
  waiting for transfers between devices  59 us (66%)
  starting transfers between devices  22.2 us (25%)
  Pallas kernels  7.44 us (8%)
    all_to_all x1, waiting for transfers between devices, per_device(): lax.all_to_all(outbox, ('sector', 'term'), split_axis=0, concat_axis=0, t...  59 us
    all_to_all x1, starting transfers between devices, per_device(): lax.all_to_all(outbox, ('sector', 'term'), split_axis=0, concat_axis=0, t...  22.2 us
    pallas_call x1, Pallas kernels, products(): pl.pallas_call(functools.partial(product_kernel, sectors, terms), in_spec...  6.23 us
  transfers between devices with their start and end apart: 1, of which 1 were waited for; matrix products, arithmetic and copies ran while one was open for 0% of the time, Pallas kernels for 0%

profile of v9, /device:TPU:1, one launch (start us, length us, event | category | flops | bytes accessed | tf_op | source)
XLA Modules:
  0.0 88.7 jit_solution(8569711102355072116)
XLA Ops:
  0.0 6.2 %shard_map.55 = f32[64,72,128]{2,1,0:T(8,128)} custom-call(s32[64]{0:T(128)} %bitcast.10, f32[64,32,128]{2,1,0:T(8,128)} %psi_hbm.1, f32[3,32,32,64]{3,2,1,0:T(8,128)} %bitcast.8, f32[3,128,128]{2,1,0:T(8,128)} %right_hbm.1), custom_call_target="tpu_custom_call" | custom-call | tf_op jit(solution)/shard_map/pallas_call | solution.py:122
  6.2 0.0 copy-start
  6.2 22.2 %all-to-all-start = ((f32[512,9,1,128]{3,2,1,0:T(1,128)}), f32[512,9,1,128]{3,2,1,0:T(1,128)S(1)}, u32[]{:S(2)}, u32[]{:S(2)}) async-start(f32[512,9,1,128]{3,2,1,0:T(1,128)} %bitcast.7), calls=%async_computation | async-start | bytes 4718592 | tf_op jit(solution)/shard_map/all_to_all | solution.py:187
  28.4 0.0 copy-done
  28.4 0.1 copy.9.live_ref
  28.5 59.0 %all-to-all-done = f32[512,9,1,128]{3,2,1,0:T(1,128)S(1)} async-done(((f32[512,9,1,128]{3,2,1,0:T(1,128)}), f32[512,9,1,128]{3,2,1,0:T(1,128)S(1)}, u32[]{:S(2)}, u32[]{:S(2)}) %all-to-all-start) | async-done | bytes 2359328 | tf_op jit(solution)/shard_map/all_to_all | solution.py:187
  87.5 1.2 %shard_map.56 = f32[64,4,128]{2,1,0:T(4,128)} custom-call(s32[1]{0:T(128)} %bitcast.term_ref, f32[4608,128]{1,0:T(8,128)S(1)} %bitcast.6, s32[64,1]{1,0:T(8,128)S(1)} %copy.9.live_ref), custom_call_target="tpu_custom_call" | custom-call | tf_op jit(solution)/shard_map/pallas_call | solution.py:173
Async XLA Ops:
  6.2 22.2 %copy-start = (s32[64]{0:T(128)S(1)}, s32[64]{0:T(128)}, u32[]{:S(2)}) copy-start(s32[64]{0:T(128)} %param.9) | copy-start | bytes 772
  6.2 81.2 %all-to-all-start = ((f32[512,9,1,128]{3,2,1,0:T(1,128)}), f32[512,9,1,128]{3,2,1,0:T(1,128)S(1)}, u32[]{:S(2)}, u32[]{:S(2)}) async-start(f32[512,9,1,128]{3,2,1,0:T(1,128)} %bitcast.7), calls=%async_computation | async-start | bytes 4718592 | tf_op jit(solution)/shard_map/all_to_all | solution.py:187

commit v10 on v8

--- a/solution.py
+++ b/solution.py
@@ -166,7 +166,7 @@
         out_specs=vmem,
         out_shape=jax.ShapeDtypeStruct((blocks, rows, cols), F32),
         scratch_shapes=[pltpu.VMEM((blocks, rows * cols), F32)],
-        compiler_params=pltpu.CompilerParams(vmem_limit_bytes=40 * 1024 * 1024),
+        compiler_params=pltpu.CompilerParams(vmem_limit_bytes=60 * 1024 * 1024),
     )(term, inbox.reshape(peers * message, cols), block_rows.reshape(blocks, 1))
 
 

time: 89.1 us -> 92.2 us (1.035)
  local copies, waits for them, and re-layouts: 0.1 us -> 2.12 us
  Pallas kernels: 7.63 us -> 9.3 us
    pallas_call x1, Pallas kernels: 1.21 us -> 2.87 us  [combine(): pl.pallas_call(functools.partial(combine_kernel, message), in_specs=[pl.B...]
    unnamed x2 -> x4, local copies, waits for them, and re-layouts: 0.01 us -> 1.43 us
  transfers between devices with their start and end apart: 1 -> 1, of which waited for: 1 -> 1; matrix products, arithmetic and copies ran while one was open for 0% -> 1% of each run, Pallas kernels for 0% -> 0%
where the time goes in v10:
time: 92.2 us; the launch traced here: 92 us
  waiting for transfers between devices  58.4 us (63%)
  starting transfers between devices  22.2 us (24%)
  Pallas kernels  9.3 us (10%)
  local copies, waits for them, and re-layouts  2.12 us (2%)
    all_to_all x1, waiting for transfers between devices, per_device(): lax.all_to_all(outbox, ('sector', 'term'), split_axis=0, concat_axis=0, t...  58.4 us
    all_to_all x1, starting transfers between devices, per_device(): lax.all_to_all(outbox, ('sector', 'term'), split_axis=0, concat_axis=0, t...  22.2 us
    pallas_call x1, Pallas kernels, products(): pl.pallas_call(functools.partial(product_kernel, sectors, terms), in_spec...  6.43 us
    pallas_call x1, Pallas kernels, combine(): pl.pallas_call(functools.partial(combine_kernel, message), in_specs=[pl.B...  2.87 us
  transfers between devices with their start and end apart: 1, of which 1 were waited for; matrix products, arithmetic and copies ran while one was open for 1% of the time, Pallas kernels for 0%

profile of v10, /device:TPU:1, one launch (start us, length us, event | category | flops | bytes accessed | tf_op | source)
XLA Modules:
  0.0 92.0 jit_solution(4042201936453779019)
XLA Ops:
  0.0 6.4 %shard_map.55 = f32[4608,128]{1,0:T(8,128)} custom-call(s32[64]{0:T(128)} %bitcast.10, f32[64,32,128]{2,1,0:T(8,128)} %psi_hbm.1, f32[3,32,32,64]{3,2,1,0:T(8,128)} %bitcast.8, f32[3,128,128]{2,1,0:T(8,128)} %right_hbm.1), custom_call_target="tpu_custom_call" | custom-call | tf_op jit(solution)/shard_map/pallas_call | solution.py:112
  6.4 0.0 copy-start.1
  6.4 22.2 %all-to-all-start = ((f32[512,9,1,128]{3,2,1,0:T(1,128)}), f32[512,9,1,128]{3,2,1,0:T(1,128)S(1)}, u32[]{:S(2)}, u32[]{:S(2)}) async-start(f32[512,9,1,128]{3,2,1,0:T(1,128)} %bitcast.7), calls=%async_computation | async-start | bytes 4718592 | tf_op jit(solution)/shard_map/all_to_all | solution.py:177
  28.6 0.0 copy-done.1
  28.6 0.7 copy.9.live_ref
  29.3 58.4 %all-to-all-done = f32[512,9,1,128]{3,2,1,0:T(1,128)S(1)} async-done(((f32[512,9,1,128]{3,2,1,0:T(1,128)}), f32[512,9,1,128]{3,2,1,0:T(1,128)S(1)}, u32[]{:S(2)}, u32[]{:S(2)}) %all-to-all-start) | async-done | bytes 2359328 | tf_op jit(solution)/shard_map/all_to_all | solution.py:177
  87.7 0.0 copy-start
  87.7 1.4 %copy-done = f32[512,9,1,128]{3,2,1,0:T(1,128)} copy-done((f32[512,9,1,128]{3,2,1,0:T(1,128)}, f32[512,9,1,128]{3,2,1,0:T(1,128)S(1)}, u32[]{:S(2)}) %copy-start) | copy-done | bytes 2359320
  89.1 2.9 %shard_map.56 = f32[64,4,128]{2,1,0:T(4,128)} custom-call(s32[1]{0:T(128)} %bitcast.term_ref, f32[4608,128]{1,0:T(8,128)} %bitcast.6, s32[64,1]{1,0:T(8,128)} %copy.9.live_ref), custom_call_target="tpu_custom_call" | custom-call | tf_op jit(solution)/shard_map/pallas_call | solution.py:163
Async XLA Ops:
  6.4 22.2 %copy-start.1 = (s32[64]{0:T(128)S(1)}, s32[64]{0:T(128)}, u32[]{:S(2)}) copy-start(s32[64]{0:T(128)} %param.9) | copy-start | bytes 772
  6.4 81.2 %all-to-all-start = ((f32[512,9,1,128]{3,2,1,0:T(1,128)}), f32[512,9,1,128]{3,2,1,0:T(1,128)S(1)}, u32[]{:S(2)}, u32[]{:S(2)}) async-start(f32[512,9,1,128]{3,2,1,0:T(1,128)} %bitcast.7), calls=%async_computation | async-start | bytes 4718592 | tf_op jit(solution)/shard_map/all_to_all | solution.py:177
  87.7 1.4 %copy-start = (f32[512,9,1,128]{3,2,1,0:T(1,128)}, f32[512,9,1,128]{3,2,1,0:T(1,128)S(1)}, u32[]{:S(2)}) copy-start(f32[512,9,1,128]{3,2,1,0:T(1,128)S(1)} %all-to-all-done) | copy-start | bytes 7077892
